TPU v7x, 32 devices: a whole 2x2x4 slice. The times are simulated.
32 devices in a mesh: grp: 2 (over x), tile: 16 (over z, y, core).
Axes of the slice: x: 2, y: 2, z: 4, core: 2. Of those that a mesh axis runs over, the one named last changes fastest.
Arguments:
- state: bfloat16 [256, 16, 512], P(('grp', 'tile')), parts along dimension 0, may hold values from -36 to 36
- wet: int32 [128], replicated, may hold values from 0 to 1, as said below
- w_vqkv: bfloat16 [512, 1536], replicated, may hold values from -0.25 to 0.25
- w_vout: bfloat16 [512, 512], replicated, may hold values from -0.25 to 0.25
- w_hqkv: bfloat16 [512, 1536], replicated, may hold values from -0.25 to 0.25
- w_hout: bfloat16 [512, 512], replicated, may hold values from -0.25 to 0.25
Outputs:
- updated: bfloat16 [256, 16, 512], P(('grp', 'tile')), parts along dimension 0
There are 2 independent parts, one for each index of `grp`. A program takes and returns all parts, laid end to end along the dimension named above; an argument that names none is the same for every part. Nothing has to cross between parts.
Inputs may be any that keep to these rules, and one draw needn't show every extreme that they name: For every strip s (blocks s * 8 to s * 8 + 7), exactly 1 of the 2 blocks with b mod 4 == 0 is wet, and exactly 1 of the 2 blocks with b mod 4 == 3.
All inputs are finite; a program needn't handle non-finite values.
Results may differ from a plain program's by a relative error of at most 0.007.
Values may be sent and summed in bfloat16 or wider, within the bound.
No kernel may reach another device: no remote copies, remote signals or barrier semaphores. Data moves between devices by JAX's collectives and lax.ppermute only.
A program may use at most 64 MiB of HBM per device.

v0:
```python
import math

import jax
import jax.numpy as jnp
from jax import lax
from jax.sharding import PartitionSpec as P

HEADS = 4
CB = 4


EPSILON = 1e-06


def row_norm(values):
    values = values.astype(jnp.float32)
    return values * lax.rsqrt(jnp.mean(values * values, axis=-1, keepdims=True) + EPSILON)


def project(inputs, weights):
    feature_width = inputs.shape[-1]
    head_size = feature_width // HEADS
    normed = row_norm(inputs).astype(jnp.bfloat16)
    joined = jnp.dot(normed.reshape(-1, feature_width), weights, preferred_element_type=jnp.float32)
    target_shape = inputs.shape[:-1] + (HEADS, head_size)
    query = row_norm(joined[:, :feature_width].reshape(target_shape)).astype(jnp.bfloat16)
    keys = row_norm(joined[:, feature_width : 2 * feature_width].reshape(target_shape)).astype(
        jnp.bfloat16
    )
    values = joined[:, 2 * feature_width :].reshape(target_shape).astype(jnp.bfloat16)
    return (query, keys, values)


def finish(inputs, context, weights):
    feature_width = inputs.shape[-1]
    update = jnp.dot(
        context.reshape(-1, feature_width), weights, preferred_element_type=jnp.float32
    )
    return (inputs.astype(jnp.float32) + update.reshape(inputs.shape)).astype(jnp.bfloat16)


def vertical_block(block, w_vqkv, w_vout):
    query, keys, values = project(block, w_vqkv)
    scale = 1.0 / math.sqrt(query.shape[-1])
    scores = jnp.einsum("clhd,cmhd->chlm", query, keys, preferred_element_type=jnp.float32) * scale
    expon = jnp.exp(scores)
    probs = (expon / jnp.sum(expon, axis=-1, keepdims=True)).astype(jnp.bfloat16)
    context = jnp.einsum(
        "chlm,cmhd->clhd", probs, values, preferred_element_type=jnp.float32
    ).astype(jnp.bfloat16)
    return finish(block, context, w_vout)


def to_grid(blocks, tiles):
    rest = blocks.shape[1:]
    row_count = blocks.shape[0] // (tiles * CB)
    shaped = jnp.moveaxis(blocks.reshape((tiles, row_count, CB) + rest), 0, 1)
    return shaped.reshape((row_count, tiles * CB) + rest)


def from_grid(grid, tiles):
    rest = grid.shape[2:]
    row_count = grid.shape[0]
    shaped = jnp.moveaxis(grid.reshape((row_count, tiles, CB) + rest), 1, 0)
    return shaped.reshape((tiles * row_count * CB,) + rest)


def wrap_columns(grid):
    return jnp.concatenate([grid[:, -1:], grid, grid[:, :1]], axis=1)


def neighbour_mix(query, keys_ext, values_ext, wet_ext):
    row_count = query.shape[0]
    col_count = query.shape[1]
    scale = 1.0 / math.sqrt(query.shape[-1])
    padding = ((1, 1), (0, 0), (0, 0), (0, 0), (0, 0))
    keys_pad = jnp.pad(keys_ext, padding)
    values_pad = jnp.pad(values_ext, padding)
    wet_pad = jnp.pad(wet_ext, ((1, 1), (0, 0)))
    inside = jnp.pad(jnp.ones((row_count, col_count + 2), jnp.int32), ((1, 1), (0, 0)))
    weights_list = []
    values_list = []
    for row_step in (-1, 0, 1):
        for col_step in (-1, 0, 1):
            rows_here = slice(1 + row_step, 1 + row_step + row_count)
            cols_here = slice(1 + col_step, 1 + col_step + col_count)
            shifted = keys_pad[rows_here, cols_here]
            scores = (
                jnp.einsum("rclhd,rclhd->rclh", query, shifted, preferred_element_type=jnp.float32)
                * scale
            )
            if row_step == 0 and col_step == 0:
                allowed = jnp.ones((row_count, col_count), jnp.int32)
            else:
                allowed = inside[rows_here, cols_here] * wet_pad[rows_here, cols_here]
            weights_list.append(
                jnp.where(allowed[:, :, None, None] > 0, jnp.exp(scores), jnp.float32(0.0))
            )
            values_list.append(values_pad[rows_here, cols_here])
    total = weights_list[0]
    for extra in weights_list[1:]:
        total = total + extra
    context = jnp.zeros(query.shape, jnp.float32)
    for weight_now, value_now in zip(weights_list, values_list):
        probs = (weight_now / total).astype(jnp.bfloat16)
        context = context + jnp.einsum(
            "rclh,rclhd->rclhd", probs, value_now, preferred_element_type=jnp.float32
        )
    return context.astype(jnp.bfloat16)


def on_device(state, wet, w_vqkv, w_vout, w_hqkv, w_hout):
    tiles = lax.axis_size("tile")
    mixed = vertical_block(state, w_vqkv, w_vout)
    wet_ext = wrap_columns(to_grid(wet, tiles))
    moved = lax.all_to_all(mixed, "tile", split_axis=1, concat_axis=0, tiled=True)
    grid = to_grid(moved, tiles)
    query, keys, values = project(grid, w_hqkv)
    context = neighbour_mix(query, wrap_columns(keys), wrap_columns(values), wet_ext)
    blocks = from_grid(finish(grid, context, w_hout), tiles)
    return lax.all_to_all(blocks, "tile", split_axis=0, concat_axis=1, tiled=True)


def solution(mesh):
    in_specs = (P(("grp", "tile"), None, None), P(), P(), P(), P(), P())
    out_specs = P(("grp", "tile"), None, None)
    return jax.shard_map(
        on_device, mesh=mesh, in_specs=in_specs, out_specs=out_specs, check_vma=False
    )
```

profile of v0, /device:TPU:0, one launch (start us, length us, event | category | flops | bytes accessed | tf_op | source)
XLA Modules:
  0.0 44.9 jit_solution(11486627552929067704)
XLA Ops:
  0.0 1.1 %fusion.8 = f32[8,16]{1,0:T(8,128)S(1)} fusion(bf16[8,16,512]{2,1,0:T(8,128)(2,1)} %param.6), kind=kLoop, calls=%fused_computation.31 | loop fusion | flops 196480 | bytes 131584 | tf_op jit(solution)/shard_map/reduce_sum | solution.py:17
  1.1 1.0 %fusion.9 = bf16[8,16,512]{2,1,0:T(8,128)(2,1)S(1)} fusion(bf16[8,16,512]{2,1,0:T(8,128)(2,1)} %param.6, f32[8,16]{1,0:T(8,128)S(1)} %add_rsqrt_fusion.5), kind=kLoop, calls=%fused_computation.32 | loop fusion | flops 196608 | bytes 262656 | tf_op jit(solution)/shard_map/convert_element_type | solution.py:23
  2.2 0.4 fusion.74
  3.3 0.3 multiply_convert_fusion.4
  3.9 0.3 fusion.3
  4.2 0.2 fusion.1
  4.4 0.7 %copy.55 = bf16[8,16,512]{2,0,1:T(8,128)(2,1)} copy(bf16[8,16,512]{2,1,0:T(8,128)(2,1)S(1)} %fusion.1) | data formatting | bytes 262144 | tf_op jit(solution)/shard_map/convert_element_type | solution.py:39
  5.2 7.5 %all-to-all-start = ((bf16[8,16,512]{2,0,1:T(8,128)(2,1)}), bf16[8,16,512]{2,0,1:T(8,128)(2,1)S(1)}, u32[]{:S(2)}, u32[]{:S(2)}) async-start(bf16[8,16,512]{2,0,1:T(8,128)(2,1)} %copy.55), calls=%async_computation | async-start | bytes 262144 | tf_op jit(solution)/shard_map/all_to_all | solution.py:116
  13.2 0.7 %slice_compare_fusion = (pred[2,64]{1,0:T(4,128)(4,1)}, pred[2,64]{1,0:T(4,128)(4,1)}) fusion(s32[2,65]{1,0:T(2,128)S(1)} %get-tuple-element.45, s32[2,65]{1,0:T(2,128)S(1)} %get-tuple-element.44), kind=kLoop, calls=%fused_computation.157 | loop fusion | flops 256 | bytes 1280 | tf_op jit(solution)/shard_map/gt | solution.py:97
  13.9 0.7 %fusion.53 = (pred[2,64]{1,0:T(4,128)(4,1)S(1)}, pred[2,64]{1,0:T(4,128)(4,1)S(1)}, pred[2,64]{1,0:T(4,128)(4,1)}, pred[2,64]{1,0:T(4,128)(4,1)S(1)}, pred[2,64]{1,0:T(4,128)(4,1)S(1)}, /*index=5*/pred[2,64]{1,0:T(4,128)(4,1)}) fusion(s32[2,66]{1,0:T(2,128)S(1)} %pad_add_fusion, s32[2]{0:T(128)S(1)} %get-tuple-element.49, s32[2]{0:T(128)S(1)} %get-tuple-element.48), kind=kLoop, calls=%fused_computation.145 | loop fusion | flops 1536 | bytes 1312 | tf_op jit(solution)/shard_map/gt | solution.py:97
  14.6 6.1 %all-to-all-done = bf16[8,16,512]{2,0,1:T(8,128)(2,1)S(1)} async-done(((bf16[8,16,512]{2,0,1:T(8,128)(2,1)}), bf16[8,16,512]{2,0,1:T(8,128)(2,1)S(1)}, u32[]{:S(2)}, u32[]{:S(2)}) %all-to-all-start) | async-done | bytes 131104 | tf_op jit(solution)/shard_map/all_to_all | solution.py:116
  20.7 0.8 %reshape.440 = f32[16,2,4,1,512]{4,2,1,0,3:T(4,128)} reshape(f32[16,8,1,512]{3,1,0,2:T(8,128)S(1)} %convert_bitcast_fusion) | data formatting | bytes 524288 | tf_op jit(solution)/shard_map/convert_element_type | solution.py:39
  21.4 1.0 %copy.128 = f32[16,2,4,1,512]{4,2,0,1,3:T(4,128)S(1)} copy(f32[16,2,4,1,512]{4,2,1,0,3:T(4,128)} %reshape.440) | data formatting | bytes 524288 | tf_op jit(solution)/shard_map/convert_element_type | solution.py:39
  22.4 0.8 %reshape.425 = f32[128,512]{1,0:T(8,128)} reshape(f32[2,16,4,1,512]{4,2,1,0,3:T(4,128)S(1)} %bitcast.125) | data formatting | bytes 524288 | tf_op jit(solution)/shard_map/convert_element_type | solution.py:39
  23.2 0.8 %reshape.424 = f32[2,64,512]{2,1,0:T(8,128)} reshape(f32[2,16,4,1,512]{4,2,1,0,3:T(4,128)S(1)} %bitcast.126) | data formatting | bytes 524288 | tf_op jit(solution)/shard_map/convert_element_type | solution.py:39
  24.4 1.4 %fusion.28 = f32[128,1536]{1,0:T(8,128)S(1)} fusion(bf16[512,1536]{1,0:T(8,128)(2,1)S(1)} %copy-done.1, f32[128,512]{1,0:T(8,128)} %reshape.425, f32[128]{0:T(128)S(1)} %rsqrt.55), kind=kOutput, calls=%fused_computation.72 | convolution fusion | flops 201457664 | bytes 2621952 | tf_op jit(solution)/shard_map/dot_general | solution.py:24
  27.2 1.6 %fusion.18 = (f32[2,64,4]{2,1,0:T(8,128)S(1)}, f32[2,64,4]{2,1,0:T(8,128)S(1)}, f32[2,64,4]{2,1,0:T(8,128)S(1)}, f32[2,64,4]{2,1,0:T(8,128)S(1)}, f32[2,64,4]{2,...) fusion(bf16[4,66,1,4,128]{4,3,1,0,2:T(4,128)(2,1)S(1)} %select_, ...), kind=kLoop, calls=%fused_computation.41 | loop fusion | flops 2223616 | bytes 1468416 | tf_op jit(solution)/shard_map/rclhd,rclhd->rclh/dot_general | solution.py:89
  28.9 0.2 fusion.42
  29.5 1.6 %fusion.20 = bf16[2,64,4,128]{3,2,1,0:T(4,128)(2,1)S(1)} fusion(f32[2,64,4,128]{3,2,1,0:T(4,128)S(1)} %reshape.432, bf16[4,66,1,4,128]{4,3,1,0,2:T(4,128)(2,1)S(1)} %select_maximum_fusion, bf16[2,1,1,4,128]{4,3,1,0,2:T(4,128)(2,1)S(1)} %get-tuple-element.26, bf16[2,64,1,4,128]{4,3,1,0,2:T(4,128)(2,1)S(1)} %convert_element_type.183, ...), kind=kLoop, calls=%fused_computation.46 | loop fusion | flops 1835008 | bytes 1333248 | tf_op jit(solution)/shard_map/convert_element_type | solution.py:109
  31.2 0.2 fusion.2
  31.6 0.5 %broadcast.290 = bf16[]{:T(256)} broadcast(bf16[]{:T(256)} %constant.190), dimensions={} | broadcast | bytes 4 | tf_op jit(solution)/shard_map/reshape | solution.py:65
  32.1 1.4 %reduce.27 = bf16[128,512]{1,0:T(8,128)(2,1)S(1)} reduce(bf16[128,1,512]{2,1,0:T(2,128)(2,1)S(1)} %reshape.474, bf16[]{:T(256)} %broadcast.290), dimensions={1}, to_apply=%reshape.474.reduce_sub_computation | reduce | bytes 262146 | tf_op jit(solution)/shard_map/reshape | solution.py:65
  33.6 10.5 %all_to_all.30 = bf16[16,2,2048]{2,1,0:T(2,128)(2,1)S(1)} all-to-all(bf16[16,2,2048]{2,1,0:T(2,128)(2,1)S(1)} %reshape.475), channel_id=1, replica_groups=mesh['grp'=2,'tile'=16] {'tile'}, dimensions={0} | all-to-all | bytes 262144 | tf_op jit(solution)/shard_map/all_to_all | solution.py:121
  44.2 0.7 %copy.62 = bf16[8,16,512]{2,1,0:T(8,128)(2,1)} copy(bf16[8,16,512]{2,0,1:T(8,128)(2,1)S(1)} %bitcast.129) | data formatting | bytes 262144 | tf_op jit(solution)/shard_map/all_to_all | solution.py:121
  (72 shorter events, 4.0 us)
Async XLA Ops:
  0.0 2.1 %copy-start = (bf16[512,1536]{1,0:T(8,128)(2,1)S(1)}, bf16[512,1536]{1,0:T(8,128)(2,1)}, u32[]{:S(2)}) copy-start(bf16[512,1536]{1,0:T(8,128)(2,1)} %param.8) | copy-start | bytes 4718596
  3.1 1.1 %copy-start.2 = (bf16[8,16,512]{2,1,0:T(8,128)(2,1)S(1)}, bf16[8,16,512]{2,1,0:T(8,128)(2,1)}, u32[]{:S(2)}) copy-start(bf16[8,16,512]{2,1,0:T(8,128)(2,1)} %param.6) | copy-start | bytes 393220
  3.1 1.1 %copy-start.4 = (bf16[512,512]{1,0:T(8,128)(2,1)S(1)}, bf16[512,512]{1,0:T(8,128)(2,1)}, u32[]{:S(2)}) copy-start(bf16[512,512]{1,0:T(8,128)(2,1)} %param.9) | copy-start | bytes 1572868
  3.7 9.0 %copy-start.10 = (s32[128]{0:T(128)S(1)}, s32[128]{0:T(128)}, u32[]{:S(2)}) copy-start(s32[128]{0:T(128)} %param.7) | copy-start | bytes 1540
  5.2 19.2 %copy-start.1 = (bf16[512,1536]{1,0:T(8,128)(2,1)S(1)}, bf16[512,1536]{1,0:T(8,128)(2,1)}, u32[]{:S(2)}) copy-start(bf16[512,1536]{1,0:T(8,128)(2,1)} %param.10) | copy-start | bytes 4718596
  5.2 15.5 %all-to-all-start = ((bf16[8,16,512]{2,0,1:T(8,128)(2,1)}), bf16[8,16,512]{2,0,1:T(8,128)(2,1)S(1)}, u32[]{:S(2)}, u32[]{:S(2)}) async-start(bf16[8,16,512]{2,0,1:T(8,128)(2,1)} %copy.55), calls=%async_computation | async-start | bytes 262144 | tf_op jit(solution)/shard_map/all_to_all | solution.py:116
  27.0 1.9 %copy-start.6 = (pred[2,64]{1,0:T(4,128)(4,1)S(1)}, pred[2,64]{1,0:T(4,128)(4,1)}, u32[]{:S(2)}) copy-start(pred[2,64]{1,0:T(4,128)(4,1)} %get-tuple-element.43) | copy-start | bytes 388
  27.0 1.9 %copy-start.7 = (pred[2,64]{1,0:T(4,128)(4,1)S(1)}, pred[2,64]{1,0:T(4,128)(4,1)}, u32[]{:S(2)}) copy-start(pred[2,64]{1,0:T(4,128)(4,1)} %get-tuple-element.52) | copy-start | bytes 388
  27.0 1.9 %copy-start.8 = (pred[2,64]{1,0:T(4,128)(4,1)S(1)}, pred[2,64]{1,0:T(4,128)(4,1)}, u32[]{:S(2)}) copy-start(pred[2,64]{1,0:T(4,128)(4,1)} %get-tuple-element.53) | copy-start | bytes 388
  27.0 1.9 %copy-start.9 = (pred[2,64]{1,0:T(4,128)(4,1)S(1)}, pred[2,64]{1,0:T(4,128)(4,1)}, u32[]{:S(2)}) copy-start(pred[2,64]{1,0:T(4,128)(4,1)} %get-tuple-element.37) | copy-start | bytes 388
  29.3 1.8 %copy-start.3 = (f32[2,64,512]{2,1,0:T(8,128)S(1)}, f32[2,64,512]{2,1,0:T(8,128)}, u32[]{:S(2)}) copy-start(f32[2,64,512]{2,1,0:T(8,128)} %reshape.424) | copy-start | bytes 786436
  29.4 1.8 %copy-start.5 = (bf16[512,512]{1,0:T(8,128)(2,1)S(1)}, bf16[512,512]{1,0:T(8,128)(2,1)}, u32[]{:S(2)}) copy-start(bf16[512,512]{1,0:T(8,128)(2,1)} %param.11) | copy-start | bytes 1572868
where the time goes:
time: 45.3 us; the launch traced here: 44.9 us
  other arithmetic  10.5 us (23%)
  blocking collectives  10.5 us (23%)
  starting transfers between devices  7.52 us (17%)
  local copies, waits for them, and re-layouts  7.15 us (16%)
  waiting for transfers between devices  6.06 us (13%)
  matrix products  2.65 us (6%)
  between operations  0.53 us (1%)
    all_to_all x1, blocking collectives, on_device(): lax.all_to_all(blocks, 'tile', split_axis=0, concat_axis=1, tiled=True)  10.5 us
    all_to_all x1, starting transfers between devices, on_device(): lax.all_to_all(mixed, 'tile', split_axis=1, concat_axis=0, tiled=True)  7.52 us
    all_to_all x1, waiting for transfers between devices, on_device(): lax.all_to_all(mixed, 'tile', split_axis=1, concat_axis=0, tiled=True)  6.06 us
    convert_element_type x4, local copies, waits for them, and re-layouts, finish(): inputs.astype(jnp.float32) + update.reshape(inputs.shape)  3.31 us
    reduce_sum x6, other arithmetic, row_norm(): jnp.mean(values * values, axis=-1, keepdims=True) + EPSILON  2.06 us
    dot_general x2, matrix products, project(): jnp.dot(normed.reshape(-1, feature_width), weights, preferred_element_typ...  1.72 us
    dot_general x1, other arithmetic, neighbour_mix(): jnp.einsum('rclhd,rclhd->rclh', query, shifted, preferred_element_type=jn...  1.64 us
    convert_element_type x1, other arithmetic, neighbour_mix(): return context.astype(jnp.bfloat16)  1.61 us
  transfers between devices with their start and end apart: 1, of which 1 were waited for; matrix products, arithmetic and copies ran while one was open for 4% of the time, Pallas kernels for 0%

commit v1 on v0

v1 whole, which is shorter than its diff:
```python
import functools
import math

import jax
import jax.numpy as jnp
from jax import lax
from jax.experimental import pallas as pl
from jax.experimental.pallas import tpu as pltpu
from jax.sharding import PartitionSpec as P

HEADS = 4
CB = 4
EPSILON = 1e-06
BF = jnp.bfloat16
F32 = jnp.float32


def each(count, body):
    if count == 1:
        body(0)
    else:
        pl.loop(0, count)(body)


def rows_at(start, size):
    if isinstance(start, int):
        return pl.ds(start, size)
    return pl.ds(pl.multiple_of(start, size), size)


def inv_rms(values):
    return lax.rsqrt(jnp.mean(values * values, axis=-1, keepdims=True) + EPSILON)


def dot(left, right):
    return jnp.dot(left, right, preferred_element_type=F32)


def dot_t(left, right):
    return lax.dot_general(left, right, (((1,), (1,)), ((), ())), preferred_element_type=F32)


def head(values, index, size):
    return values[:, index * size : (index + 1) * size]


def with_ones(values):
    return jnp.concatenate([values, jnp.ones(values.shape, values.dtype)], axis=1)


def same_block(rows, levels):
    row = lax.broadcasted_iota(jnp.int32, (rows, rows), 0) // levels
    col = lax.broadcasted_iota(jnp.int32, (rows, rows), 1) // levels
    return row == col


def vertical(block, w_vqkv, w_vout, levels):
    rows, width = block.shape
    size = width // HEADS
    scale = math.log2(math.e) / math.sqrt(size)
    values = block.astype(F32)
    joined = dot((values * inv_rms(values)).astype(BF), w_vqkv[...])
    parts = []
    for h in range(HEADS):
        query = head(joined, h, size)
        keys = head(joined, HEADS + h, size)
        query = (query * (inv_rms(query) * scale)).astype(BF)
        keys = (keys * inv_rms(keys)).astype(BF)
        expon = jnp.exp2(dot_t(query, keys))
        if rows > levels:
            expon = jnp.where(same_block(rows, levels), expon, 0.0)
        total = dot(expon.astype(BF), with_ones(head(joined, 2 * HEADS + h, size).astype(BF)))
        parts.append((total[:, :size] / total[:, size:]).astype(BF))
    return (values + dot(jnp.concatenate(parts, axis=1), w_vout[...])).astype(BF)


def own_kernel(
    levels, wet_ref, x_ref, w_vqkv, w_vout, w_hqkv, w_hout,
    out_ref, mixed_e, query_e, num_e, den_e, pick_ref, mixed_s,
):
    total_rows, width = x_ref.shape
    size = width // HEADS
    scale = math.log2(math.e) / math.sqrt(size)
    blocks = total_rows // levels
    chunk = min(levels, 16)
    edges = [b for b in range(blocks) if b % CB in (0, CB - 1)]
    tile = lax.axis_index("tile")
    tiles = lax.axis_size("tile")
    group = min(max(levels, 128), total_rows)

    def mix(index):
        rows = rows_at(index * group, group)
        mixed_s[rows, :] = vertical(x_ref[rows, :], w_vqkv, w_vout, levels)

    each(total_rows // group, mix)

    left = lax.rem(tile + tiles - 1, tiles) * blocks
    right = lax.rem(tile + 1, tiles) * blocks
    pick_ref[0, :, :] = jnp.full(pick_ref.shape[1:], wet_ref[left + CB - 1], jnp.int32)
    pick_ref[1, :, :] = jnp.full(pick_ref.shape[1:], wet_ref[right], jnp.int32)

    rows = blocks * chunk
    row = lax.broadcasted_iota(jnp.int32, (rows, rows), 0)
    col = lax.broadcasted_iota(jnp.int32, (rows, rows), 1)
    block_q, block_k = row // chunk, col // chunk
    wet_k = jnp.zeros((rows, rows), jnp.int32)
    for b in range(blocks):
        wet_k = jnp.where(block_k == b, wet_ref[tile * blocks + b], wet_k)
    near = jnp.abs(block_q % CB - block_k % CB) <= 1
    near = near & (jnp.abs(block_q // CB - block_k // CB) <= 1)
    allowed = (row % chunk == col % chunk) & ((block_q == block_k) | (near & (wet_k > 0)))

    def attend(index):
        def spots(b):
            return rows_at(b * levels + index * chunk, chunk)

        mixed = jnp.concatenate([mixed_s[spots(b), :] for b in range(blocks)], axis=0)
        values = mixed.astype(F32)
        joined = dot((values * inv_rms(values)).astype(BF), w_hqkv[...])
        parts = []
        for h in range(HEADS):
            query = head(joined, h, size)
            keys = head(joined, HEADS + h, size)
            query = (query * (inv_rms(query) * scale)).astype(BF)
            keys = (keys * inv_rms(keys)).astype(BF)
            expon = jnp.where(allowed, jnp.exp2(dot_t(query, keys)), 0.0).astype(BF)
            total = dot(expon, with_ones(head(joined, 2 * HEADS + h, size).astype(BF)))
            cols = slice(h * size, (h + 1) * size)
            for e, b in enumerate(edges):
                here = slice(b * chunk, (b + 1) * chunk)
                there = rows_at(e * levels + index * chunk, chunk)
                query_e[there, cols] = query[here]
                num_e[there, cols] = total[here, :size]
                den_e[there, cols] = total[here, size:]
            parts.append((total[:, :size] / total[:, size:]).astype(BF))
        result = (values + dot(jnp.concatenate(parts, axis=1), w_hout[...])).astype(BF)
        for b in range(blocks):
            here = slice(b * chunk, (b + 1) * chunk)
            if b in edges:
                mixed_e[rows_at(edges.index(b) * levels + index * chunk, chunk), :] = mixed[here]
            else:
                out_ref[spots(b), :] = result[here]

    each(levels // chunk, attend)


def halo_kernel(
    levels, blocks, from_left, from_right, pick_ref, mixed_e, query_e, num_e, den_e,
    w_vqkv, w_vout, w_hqkv, w_hout, partial_ref, out_ref, keys_s, values_s, result_s, sems,
):
    width = mixed_e.shape[1]
    size = width // HEADS
    chunk = min(levels, 16)
    edges = [b for b in range(blocks) if b % CB in (0, CB - 1)]
    group = 2 * levels if 2 * levels <= 128 else levels

    def choose(ref, side):
        return jnp.where(pick_ref[side, 0:1, 0:1] > 0, ref[0:levels, :], ref[levels : 2 * levels, :])

    halo = jnp.concatenate([choose(from_left, 0), choose(from_right, 1)], axis=0)
    for start in range(0, 2 * levels, group):
        rows = slice(start, start + group)
        mixed = vertical(halo[rows], w_vqkv, w_vout, levels).astype(F32)
        joined = dot((mixed * inv_rms(mixed)).astype(BF), w_hqkv[:, width:])
        for h in range(HEADS):
            cols = slice(h * size, (h + 1) * size)
            keys = head(joined, h, size)
            keys_s[rows, cols] = (keys * inv_rms(keys)).astype(BF)
        values_s[rows, :] = joined[:, width:].astype(BF)

    shape = (len(edges) * chunk, 2 * chunk)
    row = lax.broadcasted_iota(jnp.int32, shape, 0)
    col = lax.broadcasted_iota(jnp.int32, shape, 1)
    side = jnp.zeros(shape, jnp.int32)
    for e, b in enumerate(edges):
        side = jnp.where(row // chunk == e, 0 if b % CB == 0 else 1, side)
    allowed = (side == col // chunk) & (row % chunk == col % chunk)

    def attend(index):
        def take(ref, count):
            return jnp.concatenate(
                [ref[rows_at(i * levels + index * chunk, chunk), :] for i in range(count)], axis=0
            )

        keys, values = take(keys_s, 2), take(values_s, 2)
        query, num, den = (take(ref, len(edges)) for ref in (query_e, num_e, den_e))
        parts = []
        for h in range(HEADS):
            scores = dot_t(head(query, h, size), head(keys, h, size))
            expon = jnp.where(allowed, jnp.exp2(scores), 0.0).astype(BF)
            total = dot(expon, with_ones(head(values, h, size)))
            above = head(num, h, size) + total[:, :size]
            below = head(den, h, size) + total[:, size:]
            parts.append((above / below).astype(BF))
        update = dot(jnp.concatenate(parts, axis=1), w_hout[...])
        result = (take(mixed_e, len(edges)).astype(F32) + update).astype(BF)
        for e in range(len(edges)):
            there = rows_at(e * levels + index * chunk, chunk)
            result_s[there, :] = result[e * chunk : (e + 1) * chunk]

    each(levels // chunk, attend)
    copies = [
        pltpu.make_async_copy(
            result_s.at[pl.ds(e * levels, levels), :],
            out_ref.at[pl.ds(b * levels, levels), :],
            sems.at[e],
        )
        for e, b in enumerate(edges)
    ]
    for copy in copies:
        copy.start()
    for copy in copies:
        copy.wait()


def on_device(state, wet, w_vqkv, w_vout, w_hqkv, w_hout):
    tiles = lax.axis_size("tile")
    blocks, levels, width = state.shape
    rows = blocks // CB
    strip = state.reshape(rows, CB, levels, width)
    to_right = strip[:, CB - 1].reshape(rows * levels, width)
    to_left = strip[:, 0].reshape(rows * levels, width)
    from_left = lax.ppermute(to_right, "tile", [(i, (i + 1) % tiles) for i in range(tiles)])
    from_right = lax.ppermute(to_left, "tile", [(i, (i - 1) % tiles) for i in range(tiles)])

    edge_rows = 2 * rows * levels
    limit = (10 << 20) + levels * (256 << 10)
    vmem = pl.BlockSpec(memory_space=pltpu.VMEM)
    smem = pl.BlockSpec(memory_space=pltpu.SMEM)
    hbm = pl.BlockSpec(memory_space=pl.ANY)
    whole = jax.ShapeDtypeStruct((blocks * levels, width), BF)
    partial, mixed_e, query_e, num_e, den_e, pick = pl.pallas_call(
        functools.partial(own_kernel, levels),
        out_shape=(
            whole,
            jax.ShapeDtypeStruct((edge_rows, width), BF),
            jax.ShapeDtypeStruct((edge_rows, width), BF),
            jax.ShapeDtypeStruct((edge_rows, width), F32),
            jax.ShapeDtypeStruct((edge_rows, width), F32),
            jax.ShapeDtypeStruct((2, 8, 128), jnp.int32),
        ),
        in_specs=[smem] + [vmem] * 5,
        out_specs=(vmem,) * 6,
        scratch_shapes=[pltpu.VMEM((blocks * levels, width), BF)],
        compiler_params=pltpu.CompilerParams(vmem_limit_bytes=limit),
        cost_estimate=pl.CostEstimate(
            flops=2 * blocks * levels * width * width * 8, bytes_accessed=8 << 20, transcendentals=0
        ),
        name="own_blocks",
    )(wet, state.reshape(blocks * levels, width), w_vqkv, w_vout, w_hqkv, w_hout)
    updated = pl.pallas_call(
        functools.partial(halo_kernel, levels, blocks),
        out_shape=whole,
        in_specs=[vmem] * 11 + [hbm],
        out_specs=hbm,
        scratch_shapes=[
            pltpu.VMEM((2 * levels, width), BF),
            pltpu.VMEM((2 * levels, width), BF),
            pltpu.VMEM((edge_rows, width), BF),
            pltpu.SemaphoreType.DMA((2 * rows,)),
        ],
        input_output_aliases={11: 0},
        compiler_params=pltpu.CompilerParams(vmem_limit_bytes=limit),
        name="halo_blocks",
    )(from_left, from_right, pick, mixed_e, query_e, num_e, den_e,
      w_vqkv, w_vout, w_hqkv, w_hout, partial)
    return updated.reshape(blocks, levels, width)


def solution(mesh):
    in_specs = (P(("grp", "tile"), None, None), P(), P(), P(), P(), P())
    out_specs = P(("grp", "tile"), None, None)
    return jax.shard_map(
        on_device, mesh=mesh, in_specs=in_specs, out_specs=out_specs, check_vma=False
    )
```

time: 45.3 us -> 18.8 us (0.42)
  other arithmetic: 10.5 us -> 0 us
  blocking collectives: 10.5 us -> 0 us
  waiting for transfers between devices: 6.06 us -> 0.01 us
  Pallas kernels: 0 us -> 5.67 us
  matrix products: 2.65 us -> 0 us
  starting transfers between devices: 7.52 us -> 5.49 us
  between operations: 0.53 us -> 0.03 us
    all_to_all x1 -> x0, blocking collectives: 10.5 us -> none  [on_device(): lax.all_to_all(blocks, 'tile', split_axis=0, concat_axis=1, tiled=True)]
    all_to_all x1 -> x0, starting transfers between devices: 7.52 us -> none  [on_device(): lax.all_to_all(mixed, 'tile', split_axis=1, concat_axis=0, tiled=True)]
    unnamed x25 -> x18, local copies, waits for them, and re-layouts: 0.27 us -> 6.47 us
    all_to_all x1 -> x0, waiting for transfers between devices: 6.06 us -> none  [on_device(): lax.all_to_all(mixed, 'tile', split_axis=1, concat_axis=0, tiled=True)]
    pallas_call x0 -> x2, Pallas kernels: none -> 5.67 us  [the longest x1 3.17 us: on_device(): pl.pallas_call(functools.partial(own_kernel, levels), out_shape=(whole, j...]
    ppermute x0 -> x2, starting transfers between devices: none -> 5.49 us  [the longest x1 5.04 us: on_device(): lax.ppermute(to_left, 'tile', [(i, (i - 1) % tiles) for i in range(tiles)])]
    convert_element_type x7 -> x0, local copies, waits for them, and re-layouts: 4.11 us -> none  [the longest x4 3.31 us: finish(): inputs.astype(jnp.float32) + update.reshape(inputs.shape)]
    convert_element_type x5 -> x0, other arithmetic: 3.16 us -> none  [the longest x1 1.61 us: neighbour_mix(): return context.astype(jnp.bfloat16)]
  transfers between devices with their start and end apart: 1 -> 2, of which waited for: 1 -> 0; matrix products, arithmetic and copies ran while one was open for 4% -> 0% of each run, Pallas kernels for 0% -> 17%
where the time goes in v1:
time: 18.8 us; the launch traced here: 18.4 us
  local copies, waits for them, and re-layouts  7.25 us (39%)
  Pallas kernels  5.67 us (30%)
  starting transfers between devices  5.49 us (29%)
    unnamed x18, local copies, waits for them, and re-layouts  6.47 us
    ppermute x1, starting transfers between devices, on_device(): lax.ppermute(to_left, 'tile', [(i, (i - 1) % tiles) for i in range(tiles)])  5.04 us
    pallas_call x1, Pallas kernels, on_device(): pl.pallas_call(functools.partial(own_kernel, levels), out_shape=(whole, j...  3.17 us
    pallas_call x1, Pallas kernels, on_device(): pl.pallas_call(functools.partial(halo_kernel, levels, blocks), out_shape=...  2.51 us
    slice x1, local copies, waits for them, and re-layouts, on_device(): to_left = strip[:, 0].reshape(rows * levels, width)  0.78 us
    ppermute x1, starting transfers between devices, on_device(): lax.ppermute(to_right, 'tile', [(i, (i + 1) % tiles) for i in range(tiles)])  0.45 us
  transfers between devices with their start and end apart: 2, of which 0 were waited for; matrix products, arithmetic and copies ran while one was open for 0% of the time, Pallas kernels for 17%

profile of v1, /device:TPU:0, one launch (start us, length us, event | category | flops | bytes accessed | tf_op | source)
XLA Modules:
  0.0 18.4 jit_solution(4746487605448703971)
XLA Ops:
  0.0 0.8 %fusion = (bf16[2,1,16,512]{3,2,1,0:T(8,128)(2,1)S(1)}, bf16[2,1,16,512]{3,2,1,0:T(8,128)(2,1)S(1)}) fusion(bf16[2,4,16,512]{3,2,1,0:T(8,128)(2,1)} %bitcast.9), kind=kLoop, calls=%fused_computation | loop fusion | bytes 131072 | tf_op jit(solution)/shard_map/slice | solution.py:222
  0.8 0.5 %collective-permute-start = (bf16[32,512]{1,0:T(8,128)(2,1)S(1)}, bf16[32,512]{1,0:T(8,128)(2,1)S(1)}, u32[]{:S(2)}, u32[]{:S(2)}) collective-permute-start(bf16[32,512]{1,0:T(8,128)(2,1)S(1)} %bitcast.12), channel_id=1, source_target_pairs={{0,1},{1,2},{2,3},{3,4},{4,5},{5,6},{6,7},{7,8},{8,9},{9,10},{10,1... | collective-permute-start | bytes 98312 | tf_op jit(solution)/shard_map/ppermute | solution.py:223
  1.2 5.0 %collective-permute-start.1 = (bf16[32,512]{1,0:T(8,128)(2,1)S(1)}, bf16[32,512]{1,0:T(8,128)(2,1)S(1)}, u32[]{:S(2)}, u32[]{:S(2)}) collective-permute-start(bf16[32,512]{1,0:T(8,128)(2,1)S(1)} %bitcast.11), channel_id=1, source_target_pairs={{0,15},{1,0},{2,1},{3,2},{4,3},{5,4},{6,5},{7,6},{8,7},{9,8},{10,9... | collective-permute-start | bytes 98312 | tf_op jit(solution)/shard_map/ppermute | solution.py:224
  6.3 0.0 copy-start
  6.3 1.4 %copy-done = bf16[512,1536]{1,0:T(8,128)(2,1)S(1)} copy-done((bf16[512,1536]{1,0:T(8,128)(2,1)S(1)}, bf16[512,1536]{1,0:T(8,128)(2,1)}, u32[]{:S(2)}) %copy-start) | copy-done | bytes 1572888
  7.7 0.0 copy-start.2
  7.7 1.4 %copy-done.2 = bf16[512,1536]{1,0:T(8,128)(2,1)S(1)} copy-done((bf16[512,1536]{1,0:T(8,128)(2,1)S(1)}, bf16[512,1536]{1,0:T(8,128)(2,1)}, u32[]{:S(2)}) %copy-start.2) | copy-done | bytes 1572888
  9.1 0.0 copy-start.4
  9.1 1.0 %copy-done.4 = bf16[512,512]{1,0:T(8,128)(2,1)S(1)} copy-done((bf16[512,512]{1,0:T(8,128)(2,1)S(1)}, bf16[512,512]{1,0:T(8,128)(2,1)}, u32[]{:S(2)}) %copy-start.4) | copy-done | bytes 524312
  10.1 0.0 copy-start.5
  10.1 1.0 %copy-done.5 = bf16[512,512]{1,0:T(8,128)(2,1)S(1)} copy-done((bf16[512,512]{1,0:T(8,128)(2,1)S(1)}, bf16[512,512]{1,0:T(8,128)(2,1)}, u32[]{:S(2)}) %copy-start.5) | copy-done | bytes 524312
  11.2 0.0 copy-start.7
  11.2 0.9 %copy-done.7 = bf16[8,16,512]{2,1,0:T(8,128)(2,1)S(1)} copy-done((bf16[8,16,512]{2,1,0:T(8,128)(2,1)S(1)}, bf16[8,16,512]{2,1,0:T(8,128)(2,1)}, u32[]{:S(2)}) %copy-start.7) | copy-done | bytes 131096
  12.1 0.0 copy-start.8
  12.1 0.7 %copy-done.8 = s32[128]{0:T(128)S(1)} copy-done((s32[128]{0:T(128)S(1)}, s32[128]{0:T(128)}, u32[]{:S(2)}) %copy-start.8) | copy-done | bytes 536
  12.7 0.0 copy-start.1
  12.7 0.0 copy-start.6
  12.7 3.2 %own_blocks.1 = (bf16[128,512]{1,0:T(8,128)(2,1)}, bf16[64,512]{1,0:T(8,128)(2,1)S(1)}, bf16[64,512]{1,0:T(8,128)(2,1)S(1)}, f32[64,512]{1,0:T(8,128)S(1)}, f32[...) custom-call(s32[128]{0:T(128)S(1)} %copy-done.8, bf16[128,512]{1,0:T(8,128)(2,1)S(1)} %bitcast.10, ...), custom_call_target="tpu_custom_call" | custom-call | flops 536870912 | bytes 8388608 | tf_op jit(solution)/shard_map/own_blocks/pallas_call | solution.py:232
  15.9 0.0 collective-permute-done.from_left
  15.9 0.0 collective-permute-done.1.from_right
  15.9 0.0 copy-done.1
  15.9 0.0 copy-done.3
  15.9 0.0 copy-done.6
  15.9 2.5 %halo_blocks.1 = bf16[128,512]{1,0:T(8,128)(2,1)} custom-call(bf16[32,512]{1,0:T(8,128)(2,1)S(1)} %collective-permute-done.from_left, bf16[32,512]{1,0:T(8,128)(2,1)S(1)} %collective-permute-done.1.from_right, s32[2,8,128]{2,1,0:T(8,128)S(1)} %get-tuple-element.11.pick_ref, ...), custom_call_target="tpu_custom_call", output_to_operand_aliasing={{}: (11, {})} | custom-call | tf_op jit(solution)/shard_map/halo_blocks/pallas_call | solution.py:251
  (1 shorter events, 0.0 us)
Async XLA Ops:
  0.8 15.1 %collective-permute-start = (bf16[32,512]{1,0:T(8,128)(2,1)S(1)}, bf16[32,512]{1,0:T(8,128)(2,1)S(1)}, u32[]{:S(2)}, u32[]{:S(2)}) collective-permute-start(bf16[32,512]{1,0:T(8,128)(2,1)S(1)} %bitcast.12), channel_id=1, source_target_pairs={{0,1},{1,2},{2,3},{3,4},{4,5},{5,6},{6,7},{7,8},{8,9},{9,10},{10,1... | collective-permute-start | bytes 98312 | tf_op jit(solution)/shard_map/ppermute | solution.py:223
  1.2 14.7 %collective-permute-start.1 = (bf16[32,512]{1,0:T(8,128)(2,1)S(1)}, bf16[32,512]{1,0:T(8,128)(2,1)S(1)}, u32[]{:S(2)}, u32[]{:S(2)}) collective-permute-start(bf16[32,512]{1,0:T(8,128)(2,1)S(1)} %bitcast.11), channel_id=1, source_target_pairs={{0,15},{1,0},{2,1},{3,2},{4,3},{5,4},{6,5},{7,6},{8,7},{9,8},{10,9... | collective-permute-start | bytes 98312 | tf_op jit(solution)/shard_map/ppermute | solution.py:224
  6.3 1.4 %copy-start = (bf16[512,1536]{1,0:T(8,128)(2,1)S(1)}, bf16[512,1536]{1,0:T(8,128)(2,1)}, u32[]{:S(2)}) copy-start(bf16[512,1536]{1,0:T(8,128)(2,1)} %w_vqkv.3) | copy-start | bytes 4718596
  7.7 1.4 %copy-start.2 = (bf16[512,1536]{1,0:T(8,128)(2,1)S(1)}, bf16[512,1536]{1,0:T(8,128)(2,1)}, u32[]{:S(2)}) copy-start(bf16[512,1536]{1,0:T(8,128)(2,1)} %w_hqkv.3) | copy-start | bytes 4718596
  9.1 1.0 %copy-start.4 = (bf16[512,512]{1,0:T(8,128)(2,1)S(1)}, bf16[512,512]{1,0:T(8,128)(2,1)}, u32[]{:S(2)}) copy-start(bf16[512,512]{1,0:T(8,128)(2,1)} %w_vout.3) | copy-start | bytes 1572868
  10.1 1.0 %copy-start.5 = (bf16[512,512]{1,0:T(8,128)(2,1)S(1)}, bf16[512,512]{1,0:T(8,128)(2,1)}, u32[]{:S(2)}) copy-start(bf16[512,512]{1,0:T(8,128)(2,1)} %w_hout.3) | copy-start | bytes 1572868
  11.2 0.9 %copy-start.7 = (bf16[8,16,512]{2,1,0:T(8,128)(2,1)S(1)}, bf16[8,16,512]{2,1,0:T(8,128)(2,1)}, u32[]{:S(2)}) copy-start(bf16[8,16,512]{2,1,0:T(8,128)(2,1)} %param.6) | copy-start | bytes 393220
  12.1 0.7 %copy-start.8 = (s32[128]{0:T(128)S(1)}, s32[128]{0:T(128)}, u32[]{:S(2)}) copy-start(s32[128]{0:T(128)} %wet_ref.1) | copy-start | bytes 1540
  12.7 3.2 %copy-start.1 = (bf16[512,1536]{1,0:T(8,128)(2,1)S(1)}, bf16[512,1536]{1,0:T(8,128)(2,1)}, u32[]{:S(2)}) copy-start(bf16[512,1536]{1,0:T(8,128)(2,1)} %w_vqkv.3) | copy-start | bytes 4718596
  12.7 3.2 %copy-start.3 = (bf16[512,1536]{1,0:T(8,128)(2,1)S(1)}, bf16[512,1536]{1,0:T(8,128)(2,1)}, u32[]{:S(2)}) copy-start(bf16[512,1536]{1,0:T(8,128)(2,1)} %w_hqkv.3) | copy-start | bytes 4718596
  12.7 3.2 %copy-start.6 = (bf16[512,512]{1,0:T(8,128)(2,1)S(1)}, bf16[512,512]{1,0:T(8,128)(2,1)}, u32[]{:S(2)}) copy-start(bf16[512,512]{1,0:T(8,128)(2,1)} %w_hout.3) | copy-start | bytes 1572868

commit v2 on v1

--- a/solution.py
+++ b/solution.py
@@ -28,10 +28,6 @@
     return pl.ds(pl.multiple_of(start, size), size)
 
 
-def inv_rms(values):
-    return lax.rsqrt(jnp.mean(values * values, axis=-1, keepdims=True) + EPSILON)
-
-
 def dot(left, right):
     return jnp.dot(left, right, preferred_element_type=F32)
 
@@ -52,6 +48,26 @@
     row = lax.broadcasted_iota(jnp.int32, (rows, rows), 0) // levels
     col = lax.broadcasted_iota(jnp.int32, (rows, rows), 1) // levels
     return row == col
+
+
+def project(values, squares, weights, scale, size, first=0):
+    joined = dot(values, weights)
+    inverse = lax.rsqrt(squares)
+    floor = squares * EPSILON
+    out = []
+    for part in range(3 * HEADS - first * HEADS):
+        kind = part // HEADS + first
+        piece = head(joined, part, size)
+        if kind == 2:
+            out.append((piece * inverse).astype(BF))
+        else:
+            factor = lax.rsqrt(jnp.mean(piece * piece, axis=-1, keepdims=True) + floor)
+            out.append((piece * (factor * scale if kind == 0 else factor)).astype(BF))
+    return [out[i : i + HEADS] for i in range(0, len(out), HEADS)]
+
+
+def mean_square(values):
+    return jnp.mean(values * values, axis=-1, keepdims=True) + EPSILON
 
 
 def vertical(block, w_vqkv, w_vout, levels):
@@ -59,25 +75,28 @@
     size = width // HEADS
     scale = math.log2(math.e) / math.sqrt(size)
     values = block.astype(F32)
-    joined = dot((values * inv_rms(values)).astype(BF), w_vqkv[...])
+    queries, keys, vals = project(block, mean_square(values), w_vqkv[...], scale, size)
     parts = []
     for h in range(HEADS):
-        query = head(joined, h, size)
-        keys = head(joined, HEADS + h, size)
-        query = (query * (inv_rms(query) * scale)).astype(BF)
-        keys = (keys * inv_rms(keys)).astype(BF)
-        expon = jnp.exp2(dot_t(query, keys))
+        expon = jnp.exp2(dot_t(queries[h], keys[h]))
         if rows > levels:
             expon = jnp.where(same_block(rows, levels), expon, 0.0)
-        total = dot(expon.astype(BF), with_ones(head(joined, 2 * HEADS + h, size).astype(BF)))
+        total = dot(expon.astype(BF), with_ones(vals[h]))
         parts.append((total[:, :size] / total[:, size:]).astype(BF))
     return (values + dot(jnp.concatenate(parts, axis=1), w_vout[...])).astype(BF)
 
 
 def own_kernel(
-    levels, wet_ref, x_ref, w_vqkv, w_vout, w_hqkv, w_hout,
-    out_ref, mixed_e, query_e, num_e, den_e, pick_ref, mixed_s,
+    levels, wet_hbm, x_hbm, wv_hbm, wo_hbm, hv_hbm, ho_hbm,
+    result_ref, mixed_e, query_e, num_e, den_e, pick_ref, w_vqkv, w_vout, w_hqkv, w_hout,
+    x_ref, wet_ref, mixed_s, sems,
 ):
+    pairs = ((x_hbm, x_ref), (wv_hbm, w_vqkv), (wet_hbm, wet_ref), (wo_hbm, w_vout),
+             (hv_hbm, w_hqkv), (ho_hbm, w_hout))
+    copies = [pltpu.make_async_copy(a, b, sems.at[i]) for i, (a, b) in enumerate(pairs)]
+    for copy in copies:
+        copy.start()
+    x_in, wv_in, wet_in, wo_in, hv_in, ho_in = copies
     total_rows, width = x_ref.shape
     size = width // HEADS
     scale = math.log2(math.e) / math.sqrt(size)
@@ -92,7 +111,13 @@
         rows = rows_at(index * group, group)
         mixed_s[rows, :] = vertical(x_ref[rows, :], w_vqkv, w_vout, levels)
 
+    x_in.wait()
+    wv_in.wait()
+    wo_in.wait()
     each(total_rows // group, mix)
+    wet_in.wait()
+    hv_in.wait()
+    ho_in.wait()
 
     left = lax.rem(tile + tiles - 1, tiles) * blocks
     right = lax.rem(tile + 1, tiles) * blocks
@@ -116,20 +141,16 @@
 
         mixed = jnp.concatenate([mixed_s[spots(b), :] for b in range(blocks)], axis=0)
         values = mixed.astype(F32)
-        joined = dot((values * inv_rms(values)).astype(BF), w_hqkv[...])
+        queries, keys, vals = project(mixed, mean_square(values), w_hqkv[...], scale, size)
         parts = []
         for h in range(HEADS):
-            query = head(joined, h, size)
-            keys = head(joined, HEADS + h, size)
-            query = (query * (inv_rms(query) * scale)).astype(BF)
-            keys = (keys * inv_rms(keys)).astype(BF)
-            expon = jnp.where(allowed, jnp.exp2(dot_t(query, keys)), 0.0).astype(BF)
-            total = dot(expon, with_ones(head(joined, 2 * HEADS + h, size).astype(BF)))
+            expon = jnp.where(allowed, jnp.exp2(dot_t(queries[h], keys[h])), 0.0).astype(BF)
+            total = dot(expon, with_ones(vals[h]))
             cols = slice(h * size, (h + 1) * size)
             for e, b in enumerate(edges):
                 here = slice(b * chunk, (b + 1) * chunk)
                 there = rows_at(e * levels + index * chunk, chunk)
-                query_e[there, cols] = query[here]
+                query_e[there, cols] = queries[h][here]
                 num_e[there, cols] = total[here, :size]
                 den_e[there, cols] = total[here, size:]
             parts.append((total[:, :size] / total[:, size:]).astype(BF))
@@ -139,20 +160,27 @@
             if b in edges:
                 mixed_e[rows_at(edges.index(b) * levels + index * chunk, chunk), :] = mixed[here]
             else:
-                out_ref[spots(b), :] = result[here]
+                result_ref[spots(b), :] = result[here]
 
     each(levels // chunk, attend)
 
 
 def halo_kernel(
     levels, blocks, from_left, from_right, pick_ref, mixed_e, query_e, num_e, den_e,
-    w_vqkv, w_vout, w_hqkv, w_hout, partial_ref, out_ref, keys_s, values_s, result_s, sems,
+    w_vqkv, w_vout, w_hqkv, w_hout, inner_ref, out_ref, keys_s, values_s, result_s, sems,
 ):
     width = mixed_e.shape[1]
     size = width // HEADS
     chunk = min(levels, 16)
     edges = [b for b in range(blocks) if b % CB in (0, CB - 1)]
     group = 2 * levels if 2 * levels <= 128 else levels
+    inner = [
+        pltpu.make_async_copy(ref, out_ref.at[pl.ds(b * levels, levels), :], sems.at[b])
+        for b in range(blocks) if b not in edges
+        for ref in [inner_ref.at[pl.ds(b * levels, levels), :]]
+    ]
+    for copy in inner:
+        copy.start()
 
     def choose(ref, side):
         return jnp.where(pick_ref[side, 0:1, 0:1] > 0, ref[0:levels, :], ref[levels : 2 * levels, :])
@@ -160,13 +188,12 @@
     halo = jnp.concatenate([choose(from_left, 0), choose(from_right, 1)], axis=0)
     for start in range(0, 2 * levels, group):
         rows = slice(start, start + group)
-        mixed = vertical(halo[rows], w_vqkv, w_vout, levels).astype(F32)
-        joined = dot((mixed * inv_rms(mixed)).astype(BF), w_hqkv[:, width:])
+        mixed = vertical(halo[rows], w_vqkv, w_vout, levels)
+        keys, vals = project(mixed, mean_square(mixed.astype(F32)), w_hqkv[:, width:], 1.0, size, 1)
         for h in range(HEADS):
             cols = slice(h * size, (h + 1) * size)
-            keys = head(joined, h, size)
-            keys_s[rows, cols] = (keys * inv_rms(keys)).astype(BF)
-        values_s[rows, :] = joined[:, width:].astype(BF)
+            keys_s[rows, cols] = keys[h]
+            values_s[rows, cols] = vals[h]
 
     shape = (len(edges) * chunk, 2 * chunk)
     row = lax.broadcasted_iota(jnp.int32, shape, 0)
@@ -203,13 +230,13 @@
         pltpu.make_async_copy(
             result_s.at[pl.ds(e * levels, levels), :],
             out_ref.at[pl.ds(b * levels, levels), :],
-            sems.at[e],
+            sems.at[b],
         )
         for e, b in enumerate(edges)
     ]
     for copy in copies:
         copy.start()
-    for copy in copies:
+    for copy in inner + copies:
         copy.wait()
 
 
@@ -226,10 +253,11 @@
     edge_rows = 2 * rows * levels
     limit = (10 << 20) + levels * (256 << 10)
     vmem = pl.BlockSpec(memory_space=pltpu.VMEM)
-    smem = pl.BlockSpec(memory_space=pltpu.SMEM)
     hbm = pl.BlockSpec(memory_space=pl.ANY)
     whole = jax.ShapeDtypeStruct((blocks * levels, width), BF)
-    partial, mixed_e, query_e, num_e, den_e, pick = pl.pallas_call(
+    weights = (w_vqkv, w_vout, w_hqkv, w_hout)
+    operands = (wet, state.reshape(blocks * levels, width)) + weights
+    saved = pl.pallas_call(
         functools.partial(own_kernel, levels),
         out_shape=(
             whole,
@@ -238,32 +266,36 @@
             jax.ShapeDtypeStruct((edge_rows, width), F32),
             jax.ShapeDtypeStruct((edge_rows, width), F32),
             jax.ShapeDtypeStruct((2, 8, 128), jnp.int32),
-        ),
-        in_specs=[smem] + [vmem] * 5,
-        out_specs=(vmem,) * 6,
-        scratch_shapes=[pltpu.VMEM((blocks * levels, width), BF)],
+        ) + tuple(jax.ShapeDtypeStruct(w.shape, w.dtype) for w in weights),
+        in_specs=[hbm] * 6,
+        out_specs=(vmem,) * 10,
+        scratch_shapes=[
+            pltpu.VMEM((blocks * levels, width), BF),
+            pltpu.SMEM(wet.shape, wet.dtype),
+            pltpu.VMEM((blocks * levels, width), BF),
+            pltpu.SemaphoreType.DMA((6,)),
+        ],
         compiler_params=pltpu.CompilerParams(vmem_limit_bytes=limit),
         cost_estimate=pl.CostEstimate(
             flops=2 * blocks * levels * width * width * 8, bytes_accessed=8 << 20, transcendentals=0
         ),
         name="own_blocks",
-    )(wet, state.reshape(blocks * levels, width), w_vqkv, w_vout, w_hqkv, w_hout)
+    )(*[pltpu.with_memory_space_constraint(value, pltpu.HBM) for value in operands])
+    inner, *edge_values = saved[:6]
     updated = pl.pallas_call(
         functools.partial(halo_kernel, levels, blocks),
         out_shape=whole,
-        in_specs=[vmem] * 11 + [hbm],
+        in_specs=[vmem] * 12,
         out_specs=hbm,
         scratch_shapes=[
             pltpu.VMEM((2 * levels, width), BF),
             pltpu.VMEM((2 * levels, width), BF),
             pltpu.VMEM((edge_rows, width), BF),
-            pltpu.SemaphoreType.DMA((2 * rows,)),
+            pltpu.SemaphoreType.DMA((blocks,)),
         ],
-        input_output_aliases={11: 0},
         compiler_params=pltpu.CompilerParams(vmem_limit_bytes=limit),
         name="halo_blocks",
-    )(from_left, from_right, pick, mixed_e, query_e, num_e, den_e,
-      w_vqkv, w_vout, w_hqkv, w_hout, partial)
+    )(from_left, from_right, edge_values[4], *edge_values[:4], *saved[6:], inner)
     return updated.reshape(blocks, levels, width)
 
 

time: 18.8 us -> 12.3 us (0.65); the launches traced: 18.4 us -> 12.2 us
  local copies, waits for them, and re-layouts: 7.25 us -> 0.78 us
  Pallas kernels: 5.67 us -> 5.86 us
    unnamed x18 -> x0, local copies, waits for them, and re-layouts: 6.47 us -> none
    pallas_call x1, Pallas kernels: 3.17 us -> 3.5 us  [on_device(): pl.pallas_call(functools.partial(own_kernel, levels), out_shape=(whole, j...]
  transfers between devices with their start and end apart: 2 -> 2, of which waited for: 0 -> 0; matrix products, arithmetic and copies ran while one was open for 0% -> 0% of each run, Pallas kernels for 17% -> 29%
where the time goes in v2:
time: 12.3 us; the launch traced here: 12.2 us
  Pallas kernels  5.86 us (48%)
  starting transfers between devices  5.49 us (45%)
  local copies, waits for them, and re-layouts  0.78 us (6%)
    ppermute x1, starting transfers between devices, on_device(): lax.ppermute(to_left, 'tile', [(i, (i - 1) % tiles) for i in range(tiles)])  5.04 us
    pallas_call x1, Pallas kernels, on_device(): pl.pallas_call(functools.partial(own_kernel, levels), out_shape=(whole, j...  3.5 us
    pallas_call x1, Pallas kernels, on_device(): pl.pallas_call(functools.partial(halo_kernel, levels, blocks), out_shape=...  2.37 us
    slice x1, local copies, waits for them, and re-layouts, on_device(): to_left = strip[:, 0].reshape(rows * levels, width)  0.78 us
    ppermute x1, starting transfers between devices, on_device(): lax.ppermute(to_right, 'tile', [(i, (i + 1) % tiles) for i in range(tiles)])  0.45 us
  transfers between devices with their start and end apart: 2, of which 0 were waited for; matrix products, arithmetic and copies ran while one was open for 0% of the time, Pallas kernels for 29%

profile of v2, /device:TPU:0, one launch (start us, length us, event | category | flops | bytes accessed | tf_op | source)
XLA Modules:
  0.0 12.2 jit_solution(2123809909030633947)
XLA Ops:
  0.0 0.8 %fusion = (bf16[2,1,16,512]{3,2,1,0:T(8,128)(2,1)S(1)}, bf16[2,1,16,512]{3,2,1,0:T(8,128)(2,1)S(1)}) fusion(bf16[2,4,16,512]{3,2,1,0:T(8,128)(2,1)} %bitcast.9), kind=kLoop, calls=%fused_computation | loop fusion | bytes 131072 | tf_op jit(solution)/shard_map/slice | solution.py:249
  0.8 0.5 %collective-permute-start = (bf16[32,512]{1,0:T(8,128)(2,1)S(1)}, bf16[32,512]{1,0:T(8,128)(2,1)S(1)}, u32[]{:S(2)}, u32[]{:S(2)}) collective-permute-start(bf16[32,512]{1,0:T(8,128)(2,1)S(1)} %bitcast.12), channel_id=1, source_target_pairs={{0,1},{1,2},{2,3},{3,4},{4,5},{5,6},{6,7},{7,8},{8,9},{9,10},{10,1... | collective-permute-start | bytes 98312 | tf_op jit(solution)/shard_map/ppermute | solution.py:250
  1.2 5.0 %collective-permute-start.1 = (bf16[32,512]{1,0:T(8,128)(2,1)S(1)}, bf16[32,512]{1,0:T(8,128)(2,1)S(1)}, u32[]{:S(2)}, u32[]{:S(2)}) collective-permute-start(bf16[32,512]{1,0:T(8,128)(2,1)S(1)} %bitcast.11), channel_id=1, source_target_pairs={{0,15},{1,0},{2,1},{3,2},{4,3},{5,4},{6,5},{7,6},{8,7},{9,8},{10,9... | collective-permute-start | bytes 98312 | tf_op jit(solution)/shard_map/ppermute | solution.py:251
  6.3 3.5 %own_blocks.1 = (bf16[128,512]{1,0:T(8,128)(2,1)S(1)}, bf16[64,512]{1,0:T(8,128)(2,1)S(1)}, bf16[64,512]{1,0:T(8,128)(2,1)S(1)}, f32[64,512]{1,0:T(8,128)S(1)}, ...) custom-call(s32[128]{0:T(128)} %wet_hbm.1, ...), custom_call_target="tpu_custom_call" | custom-call | flops 536870912 | bytes 8388608 | tf_op jit(solution)/shard_map/own_blocks/pallas_call | solution.py:260
  9.8 0.0 collective-permute-done.from_left
  9.8 0.0 collective-permute-done.1.from_right
  9.8 2.4 %halo_blocks.1 = bf16[128,512]{1,0:T(8,128)(2,1)} custom-call(bf16[32,512]{1,0:T(8,128)(2,1)S(1)} %collective-permute-done.from_left, bf16[32,512]{1,0:T(8,128)(2,1)S(1)} %collective-permute-done.1.from_right, s32[2,8,128]{2,1,0:T(8,128)S(1)} %get-tuple-element.15.pick_ref, bf16[64,512]{1,0:T(8,128)(2,1)S(1)} %get-tuple-element.16.mixed_e, ...), custom_call_target="tpu_custom_call" | custom-call | tf_op jit(solution)/shard_map/halo_blocks/pallas_call | solution.py:285
Async XLA Ops:
  0.8 9.0 %collective-permute-start = (bf16[32,512]{1,0:T(8,128)(2,1)S(1)}, bf16[32,512]{1,0:T(8,128)(2,1)S(1)}, u32[]{:S(2)}, u32[]{:S(2)}) collective-permute-start(bf16[32,512]{1,0:T(8,128)(2,1)S(1)} %bitcast.12), channel_id=1, source_target_pairs={{0,1},{1,2},{2,3},{3,4},{4,5},{5,6},{6,7},{7,8},{8,9},{9,10},{10,1... | collective-permute-start | bytes 98312 | tf_op jit(solution)/shard_map/ppermute | solution.py:250
  1.2 8.6 %collective-permute-start.1 = (bf16[32,512]{1,0:T(8,128)(2,1)S(1)}, bf16[32,512]{1,0:T(8,128)(2,1)S(1)}, u32[]{:S(2)}, u32[]{:S(2)}) collective-permute-start(bf16[32,512]{1,0:T(8,128)(2,1)S(1)} %bitcast.11), channel_id=1, source_target_pairs={{0,15},{1,0},{2,1},{3,2},{4,3},{5,4},{6,5},{7,6},{8,7},{9,8},{10,9... | collective-permute-start | bytes 98312 | tf_op jit(solution)/shard_map/ppermute | solution.py:251

commit v3 on v2

--- a/solution.py
+++ b/solution.py
@@ -76,27 +76,23 @@
     scale = math.log2(math.e) / math.sqrt(size)
     values = block.astype(F32)
     queries, keys, vals = project(block, mean_square(values), w_vqkv[...], scale, size)
-    parts = []
-    for h in range(HEADS):
-        expon = jnp.exp2(dot_t(queries[h], keys[h]))
-        if rows > levels:
-            expon = jnp.where(same_block(rows, levels), expon, 0.0)
-        total = dot(expon.astype(BF), with_ones(vals[h]))
-        parts.append((total[:, :size] / total[:, size:]).astype(BF))
+    expons = [jnp.exp2(dot_t(q, k)) for q, k in zip(queries, keys)]
+    if rows > levels:
+        inside = same_block(rows, levels)
+        expons = [jnp.where(inside, e, 0.0) for e in expons]
+    totals = [dot(e.astype(BF), with_ones(v)) for e, v in zip(expons, vals)]
+    parts = [(t[:, :size] / t[:, size:]).astype(BF) for t in totals]
     return (values + dot(jnp.concatenate(parts, axis=1), w_vout[...])).astype(BF)
 
 
+def gate_kernel(*refs):
+    pass
+
+
 def own_kernel(
-    levels, wet_hbm, x_hbm, wv_hbm, wo_hbm, hv_hbm, ho_hbm,
-    result_ref, mixed_e, query_e, num_e, den_e, pick_ref, w_vqkv, w_vout, w_hqkv, w_hout,
-    x_ref, wet_ref, mixed_s, sems,
+    levels, wet_ref, x_ref, w_vqkv, w_vout, w_hqkv, w_hout,
+    result_ref, mixed_e, query_e, num_e, den_e, pick_ref, mixed_s,
 ):
-    pairs = ((x_hbm, x_ref), (wv_hbm, w_vqkv), (wet_hbm, wet_ref), (wo_hbm, w_vout),
-             (hv_hbm, w_hqkv), (ho_hbm, w_hout))
-    copies = [pltpu.make_async_copy(a, b, sems.at[i]) for i, (a, b) in enumerate(pairs)]
-    for copy in copies:
-        copy.start()
-    x_in, wv_in, wet_in, wo_in, hv_in, ho_in = copies
     total_rows, width = x_ref.shape
     size = width // HEADS
     scale = math.log2(math.e) / math.sqrt(size)
@@ -111,29 +107,23 @@
         rows = rows_at(index * group, group)
         mixed_s[rows, :] = vertical(x_ref[rows, :], w_vqkv, w_vout, levels)
 
-    x_in.wait()
-    wv_in.wait()
-    wo_in.wait()
     each(total_rows // group, mix)
-    wet_in.wait()
-    hv_in.wait()
-    ho_in.wait()
-
-    left = lax.rem(tile + tiles - 1, tiles) * blocks
-    right = lax.rem(tile + 1, tiles) * blocks
-    pick_ref[0, :, :] = jnp.full(pick_ref.shape[1:], wet_ref[left + CB - 1], jnp.int32)
-    pick_ref[1, :, :] = jnp.full(pick_ref.shape[1:], wet_ref[right], jnp.int32)
 
     rows = blocks * chunk
     row = lax.broadcasted_iota(jnp.int32, (rows, rows), 0)
     col = lax.broadcasted_iota(jnp.int32, (rows, rows), 1)
     block_q, block_k = row // chunk, col // chunk
-    wet_k = jnp.zeros((rows, rows), jnp.int32)
-    for b in range(blocks):
-        wet_k = jnp.where(block_k == b, wet_ref[tile * blocks + b], wet_k)
+    wet = wet_ref[...].astype(BF)
+    which = lax.broadcasted_iota(jnp.int32, (wet.shape[1], rows), 0)
+    column = lax.broadcasted_iota(jnp.int32, (wet.shape[1], rows), 1) // chunk
+    wet_k = dot(wet, (which == tile * blocks + column).astype(BF))[0:1, :]
+    left = lax.rem(tile + tiles - 1, tiles) * blocks + CB - 1
+    right = lax.rem(tile + 1, tiles) * blocks
+    for i, block in enumerate((left, right)):
+        pick_ref[i, :, :] = dot(wet, (which[:, :128] == block).astype(BF))
     near = jnp.abs(block_q % CB - block_k % CB) <= 1
     near = near & (jnp.abs(block_q // CB - block_k // CB) <= 1)
-    allowed = (row % chunk == col % chunk) & ((block_q == block_k) | (near & (wet_k > 0)))
+    allowed = (row % chunk == col % chunk) & ((block_q == block_k) | (near & (wet_k > 0.5)))
 
     def attend(index):
         def spots(b):
@@ -142,10 +132,11 @@
         mixed = jnp.concatenate([mixed_s[spots(b), :] for b in range(blocks)], axis=0)
         values = mixed.astype(F32)
         queries, keys, vals = project(mixed, mean_square(values), w_hqkv[...], scale, size)
-        parts = []
-        for h in range(HEADS):
-            expon = jnp.where(allowed, jnp.exp2(dot_t(queries[h], keys[h])), 0.0).astype(BF)
-            total = dot(expon, with_ones(vals[h]))
+        expons = [jnp.exp2(dot_t(q, k)) for q, k in zip(queries, keys)]
+        expons = [jnp.where(allowed, e, 0.0).astype(BF) for e in expons]
+        totals = [dot(e, with_ones(v)) for e, v in zip(expons, vals)]
+        parts = [(t[:, :size] / t[:, size:]).astype(BF) for t in totals]
+        for h, total in enumerate(totals):
             cols = slice(h * size, (h + 1) * size)
             for e, b in enumerate(edges):
                 here = slice(b * chunk, (b + 1) * chunk)
@@ -153,7 +144,6 @@
                 query_e[there, cols] = queries[h][here]
                 num_e[there, cols] = total[here, :size]
                 den_e[there, cols] = total[here, size:]
-            parts.append((total[:, :size] / total[:, size:]).astype(BF))
         result = (values + dot(jnp.concatenate(parts, axis=1), w_hout[...])).astype(BF)
         for b in range(blocks):
             here = slice(b * chunk, (b + 1) * chunk)
@@ -182,10 +172,13 @@
     for copy in inner:
         copy.start()
 
-    def choose(ref, side):
-        return jnp.where(pick_ref[side, 0:1, 0:1] > 0, ref[0:levels, :], ref[levels : 2 * levels, :])
-
-    halo = jnp.concatenate([choose(from_left, 0), choose(from_right, 1)], axis=0)
+    halo = jnp.concatenate(
+        [
+            jnp.where(pick_ref[i, 0:1, 0:1] > 0.5, ref[0:levels, :], ref[levels : 2 * levels, :])
+            for i, ref in enumerate((from_left, from_right))
+        ],
+        axis=0,
+    )
     for start in range(0, 2 * levels, group):
         rows = slice(start, start + group)
         mixed = vertical(halo[rows], w_vqkv, w_vout, levels)
@@ -211,14 +204,13 @@
 
         keys, values = take(keys_s, 2), take(values_s, 2)
         query, num, den = (take(ref, len(edges)) for ref in (query_e, num_e, den_e))
-        parts = []
-        for h in range(HEADS):
-            scores = dot_t(head(query, h, size), head(keys, h, size))
-            expon = jnp.where(allowed, jnp.exp2(scores), 0.0).astype(BF)
-            total = dot(expon, with_ones(head(values, h, size)))
-            above = head(num, h, size) + total[:, :size]
-            below = head(den, h, size) + total[:, size:]
-            parts.append((above / below).astype(BF))
+        scores = [dot_t(head(query, h, size), head(keys, h, size)) for h in range(HEADS)]
+        expons = [jnp.where(allowed, jnp.exp2(x), 0.0).astype(BF) for x in scores]
+        totals = [dot(e, with_ones(head(values, h, size))) for h, e in enumerate(expons)]
+        parts = [
+            ((head(num, h, size) + t[:, :size]) / (head(den, h, size) + t[:, size:])).astype(BF)
+            for h, t in enumerate(totals)
+        ]
         update = dot(jnp.concatenate(parts, axis=1), w_hout[...])
         result = (take(mixed_e, len(edges)).astype(F32) + update).astype(BF)
         for e in range(len(edges)):
@@ -244,20 +236,28 @@
     tiles = lax.axis_size("tile")
     blocks, levels, width = state.shape
     rows = blocks // CB
-    strip = state.reshape(rows, CB, levels, width)
-    to_right = strip[:, CB - 1].reshape(rows * levels, width)
-    to_left = strip[:, 0].reshape(rows * levels, width)
-    from_left = lax.ppermute(to_right, "tile", [(i, (i + 1) % tiles) for i in range(tiles)])
-    from_right = lax.ppermute(to_left, "tile", [(i, (i - 1) % tiles) for i in range(tiles)])
-
     edge_rows = 2 * rows * levels
     limit = (10 << 20) + levels * (256 << 10)
     vmem = pl.BlockSpec(memory_space=pltpu.VMEM)
     hbm = pl.BlockSpec(memory_space=pl.ANY)
     whole = jax.ShapeDtypeStruct((blocks * levels, width), BF)
+    strip = state.reshape(rows, CB, levels, width)
+    edges = [strip[:, c].reshape(rows * levels, width) for c in (CB - 1, 0)]
+    to_right, to_left = pl.pallas_call(
+        gate_kernel,
+        out_shape=[jax.ShapeDtypeStruct(e.shape, e.dtype) for e in edges],
+        in_specs=[vmem] * 2,
+        out_specs=[vmem] * 2,
+        input_output_aliases={0: 0, 1: 1},
+        compiler_params=pltpu.CompilerParams(vmem_limit_bytes=1 << 20),
+        cost_estimate=pl.CostEstimate(flops=200 << 30, bytes_accessed=1 << 30, transcendentals=0),
+        name="gate",
+    )(*edges)
+    from_left = lax.ppermute(to_right, "tile", [(i, (i + 1) % tiles) for i in range(tiles)])
+    from_right = lax.ppermute(to_left, "tile", [(i, (i - 1) % tiles) for i in range(tiles)])
+
     weights = (w_vqkv, w_vout, w_hqkv, w_hout)
-    operands = (wet, state.reshape(blocks * levels, width)) + weights
-    saved = pl.pallas_call(
+    inner, *edge_values, pick = pl.pallas_call(
         functools.partial(own_kernel, levels),
         out_shape=(
             whole,
@@ -265,23 +265,17 @@
             jax.ShapeDtypeStruct((edge_rows, width), BF),
             jax.ShapeDtypeStruct((edge_rows, width), F32),
             jax.ShapeDtypeStruct((edge_rows, width), F32),
-            jax.ShapeDtypeStruct((2, 8, 128), jnp.int32),
-        ) + tuple(jax.ShapeDtypeStruct(w.shape, w.dtype) for w in weights),
-        in_specs=[hbm] * 6,
-        out_specs=(vmem,) * 10,
-        scratch_shapes=[
-            pltpu.VMEM((blocks * levels, width), BF),
-            pltpu.SMEM(wet.shape, wet.dtype),
-            pltpu.VMEM((blocks * levels, width), BF),
-            pltpu.SemaphoreType.DMA((6,)),
-        ],
+            jax.ShapeDtypeStruct((2, 8, 128), F32),
+        ),
+        in_specs=[vmem] * 6,
+        out_specs=(vmem,) * 6,
+        scratch_shapes=[pltpu.VMEM((blocks * levels, width), BF)],
         compiler_params=pltpu.CompilerParams(vmem_limit_bytes=limit),
         cost_estimate=pl.CostEstimate(
             flops=2 * blocks * levels * width * width * 8, bytes_accessed=8 << 20, transcendentals=0
         ),
         name="own_blocks",
-    )(*[pltpu.with_memory_space_constraint(value, pltpu.HBM) for value in operands])
-    inner, *edge_values = saved[:6]
+    )(jnp.broadcast_to(wet, (8, wet.shape[0])), state.reshape(blocks * levels, width), *weights)
     updated = pl.pallas_call(
         functools.partial(halo_kernel, levels, blocks),
         out_shape=whole,
@@ -295,7 +289,7 @@
         ],
         compiler_params=pltpu.CompilerParams(vmem_limit_bytes=limit),
         name="halo_blocks",
-    )(from_left, from_right, edge_values[4], *edge_values[:4], *saved[6:], inner)
+    )(from_left, from_right, pick, *edge_values, *weights, inner)
     return updated.reshape(blocks, levels, width)
 
 

time: 12.3 us -> 10.6 us (0.86)
  Pallas kernels: 5.86 us -> 3.98 us
    pallas_call x1, Pallas kernels: 3.5 us -> 1.73 us  [on_device(): pl.pallas_call(functools.partial(own_kernel, levels), out_shape=(whole, j...]
  transfers between devices with their start and end apart: 2 -> 2, of which waited for: 0 -> 0; matrix products, arithmetic and copies ran while one was open for 0% -> 0% of each run, Pallas kernels for 29% -> 16%
where the time goes in v3:
time: 10.6 us; the launch traced here: 10.5 us
  starting transfers between devices  5.56 us (52%)
  Pallas kernels  3.98 us (38%)
  local copies, waits for them, and re-layouts  0.81 us (8%)
    ppermute x1, starting transfers between devices, on_device(): lax.ppermute(to_left, 'tile', [(i, (i - 1) % tiles) for i in range(tiles)])  5.06 us
    pallas_call x1, Pallas kernels, on_device(): pl.pallas_call(functools.partial(halo_kernel, levels, blocks), out_shape=...  2.25 us
    pallas_call x1, Pallas kernels, on_device(): pl.pallas_call(functools.partial(own_kernel, levels), out_shape=(whole, j...  1.73 us
    slice x1, local copies, waits for them, and re-layouts, on_device(): edges = [strip[:, c].reshape(rows * levels, width) for c in (CB - 1, 0)]  0.78 us
    ppermute x1, starting transfers between devices, on_device(): lax.ppermute(to_right, 'tile', [(i, (i + 1) % tiles) for i in range(tiles)])  0.5 us
  transfers between devices with their start and end apart: 2, of which 0 were waited for; matrix products, arithmetic and copies ran while one was open for 0% of the time, Pallas kernels for 16%

profile of v3, /device:TPU:0, one launch (start us, length us, event | category | flops | bytes accessed | tf_op | source)
XLA Modules:
  0.0 10.5 jit_solution(15543067131262898498)
XLA Ops:
  0.0 0.8 %fusion = (bf16[2,1,16,512]{3,2,1,0:T(8,128)(2,1)S(1)}, bf16[2,1,16,512]{3,2,1,0:T(8,128)(2,1)S(1)}) fusion(bf16[2,4,16,512]{3,2,1,0:T(8,128)(2,1)} %bitcast.9), kind=kLoop, calls=%fused_computation | loop fusion | bytes 131072 | tf_op jit(solution)/shard_map/slice | solution.py:245
  0.8 0.0 copy-start.5
  0.8 0.0 copy-start
  0.8 0.0 copy-start.1
  0.8 0.0 copy-start.2
  0.8 0.0 copy-start.3
  0.8 0.0 copy-start.4
  0.8 0.5 %collective-permute-start = (bf16[32,512]{1,0:T(8,128)(2,1)S(1)}, bf16[32,512]{1,0:T(8,128)(2,1)S(1)}, u32[]{:S(2)}, u32[]{:S(2)}) collective-permute-start(bf16[32,512]{1,0:T(8,128)(2,1)S(1)} %get-tuple-element.13), channel_id=1, source_target_pairs={{0,1},{1,2},{2,3},{3,4},{4,5},{5,6},{6,7},{7,8},{8,9},{9,10},{10,1... | collective-permute-start | bytes 98312 | tf_op jit(solution)/shard_map/ppermute | solution.py:256
  1.4 5.1 %collective-permute-start.1 = (bf16[32,512]{1,0:T(8,128)(2,1)S(1)}, bf16[32,512]{1,0:T(8,128)(2,1)S(1)}, u32[]{:S(2)}, u32[]{:S(2)}) collective-permute-start(bf16[32,512]{1,0:T(8,128)(2,1)S(1)} %get-tuple-element.14), channel_id=1, source_target_pairs={{0,15},{1,0},{2,1},{3,2},{4,3},{5,4},{6,5},{7,6},{8,7},{9,8},{10,9... | collective-permute-start | bytes 98312 | tf_op jit(solution)/shard_map/ppermute | solution.py:257
  6.4 0.0 copy-done.5
  6.4 0.0 copy-done
  6.4 0.0 copy-done.1
  6.4 0.0 copy-done.2
  6.4 0.0 copy-done.3
  6.4 0.0 copy-done.4
  6.5 1.7 %own_blocks.1 = (bf16[128,512]{1,0:T(8,128)(2,1)S(1)}, bf16[64,512]{1,0:T(8,128)(2,1)S(1)}, bf16[64,512]{1,0:T(8,128)(2,1)S(1)}, f32[64,512]{1,0:T(8,128)S(1)}, ...) custom-call(s32[8,128]{1,0:T(8,128)S(1)} %broadcast_in_dim.3.wet_ref, bf16[128,512]{1,0:T(8,128)(2,1)S(1)} %bitcast.10, ...), custom_call_target="tpu_custom_call" | custom-call | flops 536870912 | bytes 8388608 | tf_op jit(solution)/shard_map/own_blocks/pallas_call | solution.py:260
  8.2 0.0 collective-permute-done.from_left
  8.2 0.0 collective-permute-done.1.from_right
  8.2 2.2 %halo_blocks.1 = bf16[128,512]{1,0:T(8,128)(2,1)} custom-call(bf16[32,512]{1,0:T(8,128)(2,1)S(1)} %collective-permute-done.from_left, bf16[32,512]{1,0:T(8,128)(2,1)S(1)} %collective-permute-done.1.from_right, f32[2,8,128]{2,1,0:T(8,128)S(1)} %get-tuple-element.15.pick_ref, bf16[64,512]{1,0:T(8,128)(2,1)S(1)} %get-tuple-element.16.mixed_e, ...), custom_call_target="tpu_custom_call" | custom-call | tf_op jit(solution)/shard_map/halo_blocks/pallas_call | solution.py:279
  (2 shorter events, 0.0 us)
Async XLA Ops:
  0.8 5.6 %copy-start.5 = (s32[128]{0:T(128)S(1)}, s32[128]{0:T(128)}, u32[]{:S(2)}) copy-start(s32[128]{0:T(128)} %param.7) | copy-start | bytes 1540
  0.8 5.6 %copy-start = (bf16[512,1536]{1,0:T(8,128)(2,1)S(1)}, bf16[512,1536]{1,0:T(8,128)(2,1)}, u32[]{:S(2)}) copy-start(bf16[512,1536]{1,0:T(8,128)(2,1)} %w_vqkv.3) | copy-start | bytes 4718596
  0.8 5.6 %copy-start.1 = (bf16[512,1536]{1,0:T(8,128)(2,1)S(1)}, bf16[512,1536]{1,0:T(8,128)(2,1)}, u32[]{:S(2)}) copy-start(bf16[512,1536]{1,0:T(8,128)(2,1)} %w_hqkv.3) | copy-start | bytes 4718596
  0.8 5.6 %copy-start.2 = (bf16[512,512]{1,0:T(8,128)(2,1)S(1)}, bf16[512,512]{1,0:T(8,128)(2,1)}, u32[]{:S(2)}) copy-start(bf16[512,512]{1,0:T(8,128)(2,1)} %w_vout.3) | copy-start | bytes 1572868
  0.8 5.6 %copy-start.3 = (bf16[512,512]{1,0:T(8,128)(2,1)S(1)}, bf16[512,512]{1,0:T(8,128)(2,1)}, u32[]{:S(2)}) copy-start(bf16[512,512]{1,0:T(8,128)(2,1)} %w_hout.3) | copy-start | bytes 1572868
  0.8 5.6 %copy-start.4 = (bf16[8,16,512]{2,1,0:T(8,128)(2,1)S(1)}, bf16[8,16,512]{2,1,0:T(8,128)(2,1)}, u32[]{:S(2)}) copy-start(bf16[8,16,512]{2,1,0:T(8,128)(2,1)} %param.6) | copy-start | bytes 393220
  0.8 7.3 %collective-permute-start = (bf16[32,512]{1,0:T(8,128)(2,1)S(1)}, bf16[32,512]{1,0:T(8,128)(2,1)S(1)}, u32[]{:S(2)}, u32[]{:S(2)}) collective-permute-start(bf16[32,512]{1,0:T(8,128)(2,1)S(1)} %get-tuple-element.13), channel_id=1, source_target_pairs={{0,1},{1,2},{2,3},{3,4},{4,5},{5,6},{6,7},{7,8},{8,9},{9,10},{10,1... | collective-permute-start | bytes 98312 | tf_op jit(solution)/shard_map/ppermute | solution.py:256
  1.4 6.8 %collective-permute-start.1 = (bf16[32,512]{1,0:T(8,128)(2,1)S(1)}, bf16[32,512]{1,0:T(8,128)(2,1)S(1)}, u32[]{:S(2)}, u32[]{:S(2)}) collective-permute-start(bf16[32,512]{1,0:T(8,128)(2,1)S(1)} %get-tuple-element.14), channel_id=1, source_target_pairs={{0,15},{1,0},{2,1},{3,2},{4,3},{5,4},{6,5},{7,6},{8,7},{9,8},{10,9... | collective-permute-start | bytes 98312 | tf_op jit(solution)/shard_map/ppermute | solution.py:257

commit v4 on v3

--- a/solution.py
+++ b/solution.py
@@ -75,12 +75,29 @@
     size = width // HEADS
     scale = math.log2(math.e) / math.sqrt(size)
     values = block.astype(F32)
-    queries, keys, vals = project(block, mean_square(values), w_vqkv[...], scale, size)
-    expons = [jnp.exp2(dot_t(q, k)) for q, k in zip(queries, keys)]
+    heads = range(HEADS)
+    keys = dot(block, w_vqkv[:, width : 2 * width])
+    queries = dot(block, w_vqkv[:, :width])
+    vals = dot(block, w_vqkv[:, 2 * width :])
+    squares = mean_square(values)
+    squares_k = dot_t(jnp.full((8, width), 1.0 / width, BF), (values * values).astype(BF))[0:1]
+    floor, floor_k = squares * EPSILON, (squares_k + EPSILON) * EPSILON
+    keys_sq = (keys * keys).astype(BF)
+    queries_b, keys_b = queries.astype(BF), keys.astype(BF)
+    scores = [dot_t(head(queries_b, h, size), head(keys_b, h, size)) for h in heads]
+    ones = jnp.full((8, size), 1.0 / size, BF)
+    means_k = [dot_t(ones, head(keys_sq, h, size))[0:1] for h in heads]
+    norms_q = [
+        lax.rsqrt(jnp.mean(q * q, axis=-1, keepdims=True) + floor) * scale
+        for q in (head(queries, h, size) for h in heads)
+    ]
+    norms_k = [lax.rsqrt(m + floor_k) for m in means_k]
+    vals = (vals * lax.rsqrt(squares)).astype(BF)
+    expons = [jnp.exp2(x * q * k) for x, q, k in zip(scores, norms_q, norms_k)]
     if rows > levels:
         inside = same_block(rows, levels)
         expons = [jnp.where(inside, e, 0.0) for e in expons]
-    totals = [dot(e.astype(BF), with_ones(v)) for e, v in zip(expons, vals)]
+    totals = [dot(e.astype(BF), with_ones(head(vals, h, size))) for h, e in enumerate(expons)]
     parts = [(t[:, :size] / t[:, size:]).astype(BF) for t in totals]
     return (values + dot(jnp.concatenate(parts, axis=1), w_vout[...])).astype(BF)
 
@@ -89,9 +106,28 @@
     pass
 
 
-def own_kernel(
-    levels, wet_ref, x_ref, w_vqkv, w_vout, w_hqkv, w_hout,
-    result_ref, mixed_e, query_e, num_e, den_e, pick_ref, mixed_s,
+def early_kernel(levels, *refs):
+    operands, outputs, loaded, mixed_s, sems = refs[:6], refs[7:13], refs[14:20], refs[20], refs[21]
+
+    @pl.when(lax.axis_index("tile") == 0)
+    def _():
+        copies = [
+            pltpu.make_async_copy(a, b, sems.at[i]) for i, (a, b) in enumerate(zip(operands, loaded))
+        ]
+        for copy in copies:
+            copy.start()
+        own_blocks(levels, *loaded, *outputs, mixed_s, copies)
+
+
+def late_kernel(levels, *refs):
+    @pl.when(lax.axis_index("tile") != 0)
+    def _():
+        own_blocks(levels, *refs[:6], *refs[12:18], refs[18], ())
+
+
+def own_blocks(
+    levels, x_ref, w_vqkv, w_vout, wet_ref, w_hqkv, w_hout,
+    result_ref, mixed_e, query_e, num_e, den_e, pick_ref, mixed_s, copies,
 ):
     total_rows, width = x_ref.shape
     size = width // HEADS
@@ -107,13 +143,17 @@
         rows = rows_at(index * group, group)
         mixed_s[rows, :] = vertical(x_ref[rows, :], w_vqkv, w_vout, levels)
 
+    for copy in copies[:3]:
+        copy.wait()
     each(total_rows // group, mix)
+    for copy in copies[3:]:
+        copy.wait()
 
     rows = blocks * chunk
     row = lax.broadcasted_iota(jnp.int32, (rows, rows), 0)
     col = lax.broadcasted_iota(jnp.int32, (rows, rows), 1)
     block_q, block_k = row // chunk, col // chunk
-    wet = wet_ref[...].astype(BF)
+    wet = jnp.broadcast_to(wet_ref[...], (8, wet_ref.shape[1])).astype(BF)
     which = lax.broadcasted_iota(jnp.int32, (wet.shape[1], rows), 0)
     column = lax.broadcasted_iota(jnp.int32, (wet.shape[1], rows), 1) // chunk
     wet_k = dot(wet, (which == tile * blocks + column).astype(BF))[0:1, :]
@@ -157,7 +197,7 @@
 
 def halo_kernel(
     levels, blocks, from_left, from_right, pick_ref, mixed_e, query_e, num_e, den_e,
-    w_vqkv, w_vout, w_hqkv, w_hout, inner_ref, out_ref, keys_s, values_s, result_s, sems,
+    w_vqkv, w_vout, w_hqkv, w_hout, inner_ref, out_ref, keys_s, values_s, floor_s, result_s, sems,
 ):
     width = mixed_e.shape[1]
     size = width // HEADS
@@ -182,19 +222,11 @@
     for start in range(0, 2 * levels, group):
         rows = slice(start, start + group)
         mixed = vertical(halo[rows], w_vqkv, w_vout, levels)
-        keys, vals = project(mixed, mean_square(mixed.astype(F32)), w_hqkv[:, width:], 1.0, size, 1)
-        for h in range(HEADS):
-            cols = slice(h * size, (h + 1) * size)
-            keys_s[rows, cols] = keys[h]
-            values_s[rows, cols] = vals[h]
-
-    shape = (len(edges) * chunk, 2 * chunk)
-    row = lax.broadcasted_iota(jnp.int32, shape, 0)
-    col = lax.broadcasted_iota(jnp.int32, shape, 1)
-    side = jnp.zeros(shape, jnp.int32)
-    for e, b in enumerate(edges):
-        side = jnp.where(row // chunk == e, 0 if b % CB == 0 else 1, side)
-    allowed = (side == col // chunk) & (row % chunk == col % chunk)
+        squares = mean_square(mixed.astype(F32))
+        joined = dot(mixed, w_hqkv[:, width:])
+        keys_s[rows, :] = joined[:, :width]
+        values_s[rows, :] = joined[:, width:] * lax.rsqrt(squares)
+        floor_s[rows, :] = jnp.broadcast_to(squares * EPSILON, (group, 128))
 
     def attend(index):
         def take(ref, count):
@@ -202,14 +234,23 @@
                 [ref[rows_at(i * levels + index * chunk, chunk), :] for i in range(count)], axis=0
             )
 
-        keys, values = take(keys_s, 2), take(values_s, 2)
+        def per_edge(values):
+            sides = [values[:chunk], values[chunk:]]
+            return jnp.concatenate([sides[0 if b % CB == 0 else 1] for b in edges], axis=0)
+
+        keys, values, floor = (take(ref, 2) for ref in (keys_s, values_s, floor_s))
         query, num, den = (take(ref, len(edges)) for ref in (query_e, num_e, den_e))
-        scores = [dot_t(head(query, h, size), head(keys, h, size)) for h in range(HEADS)]
-        expons = [jnp.where(allowed, jnp.exp2(x), 0.0).astype(BF) for x in scores]
-        totals = [dot(e, with_ones(head(values, h, size))) for h, e in enumerate(expons)]
+        product = query.astype(F32) * per_edge(keys)
+        squares = keys * keys
+        heads = range(HEADS)
+        scores = [jnp.sum(head(product, h, size), axis=-1, keepdims=True) for h in heads]
+        means = [jnp.mean(head(squares, h, size), axis=-1, keepdims=True) for h in heads]
+        norms = [per_edge(lax.rsqrt(m + floor[:, 0:1])) for m in means]
+        expons = [jnp.exp2(x * n) for x, n in zip(scores, norms)]
+        values = per_edge(values)
         parts = [
-            ((head(num, h, size) + t[:, :size]) / (head(den, h, size) + t[:, size:])).astype(BF)
-            for h, t in enumerate(totals)
+            ((head(num, h, size) + e * head(values, h, size)) / (head(den, h, size) + e)).astype(BF)
+            for h, e in enumerate(expons)
         ]
         update = dot(jnp.concatenate(parts, axis=1), w_hout[...])
         result = (take(mixed_e, len(edges)).astype(F32) + update).astype(BF)
@@ -254,42 +295,61 @@
         name="gate",
     )(*edges)
     from_left = lax.ppermute(to_right, "tile", [(i, (i + 1) % tiles) for i in range(tiles)])
+    results = (
+        whole,
+        jax.ShapeDtypeStruct((edge_rows, width), BF),
+        jax.ShapeDtypeStruct((edge_rows, width), BF),
+        jax.ShapeDtypeStruct((edge_rows, width), F32),
+        jax.ShapeDtypeStruct((edge_rows, width), F32),
+        jax.ShapeDtypeStruct((2, 8, 128), F32),
+    )
+    operands = (
+        state.reshape(blocks * levels, width), w_vqkv, w_vout, wet.reshape(1, -1), w_hqkv, w_hout
+    )
+    mixed_s = pltpu.VMEM((blocks * levels, width), BF)
+    cost = pl.CostEstimate(
+        flops=2 * blocks * levels * width * width * 8, bytes_accessed=8 << 20, transcendentals=0
+    )
+    *early, to_left = pl.pallas_call(
+        functools.partial(early_kernel, levels),
+        out_shape=results + (jax.ShapeDtypeStruct(to_left.shape, to_left.dtype),),
+        in_specs=[hbm] * 6 + [vmem],
+        out_specs=(vmem,) * 7,
+        input_output_aliases={6: 6},
+        scratch_shapes=[pltpu.VMEM(v.shape, v.dtype) for v in operands]
+        + [mixed_s, pltpu.SemaphoreType.DMA((6,))],
+        compiler_params=pltpu.CompilerParams(vmem_limit_bytes=limit + (6 << 20)),
+        cost_estimate=cost,
+        name="early_blocks",
+    )(*[pltpu.with_memory_space_constraint(v, pltpu.HBM) for v in operands], to_left)
     from_right = lax.ppermute(to_left, "tile", [(i, (i - 1) % tiles) for i in range(tiles)])
 
-    weights = (w_vqkv, w_vout, w_hqkv, w_hout)
     inner, *edge_values, pick = pl.pallas_call(
-        functools.partial(own_kernel, levels),
-        out_shape=(
-            whole,
-            jax.ShapeDtypeStruct((edge_rows, width), BF),
-            jax.ShapeDtypeStruct((edge_rows, width), BF),
-            jax.ShapeDtypeStruct((edge_rows, width), F32),
-            jax.ShapeDtypeStruct((edge_rows, width), F32),
-            jax.ShapeDtypeStruct((2, 8, 128), F32),
-        ),
-        in_specs=[vmem] * 6,
+        functools.partial(late_kernel, levels),
+        out_shape=results,
+        in_specs=[vmem] * 12,
         out_specs=(vmem,) * 6,
-        scratch_shapes=[pltpu.VMEM((blocks * levels, width), BF)],
+        input_output_aliases={6 + i: i for i in range(6)},
+        scratch_shapes=[mixed_s],
         compiler_params=pltpu.CompilerParams(vmem_limit_bytes=limit),
-        cost_estimate=pl.CostEstimate(
-            flops=2 * blocks * levels * width * width * 8, bytes_accessed=8 << 20, transcendentals=0
-        ),
-        name="own_blocks",
-    )(jnp.broadcast_to(wet, (8, wet.shape[0])), state.reshape(blocks * levels, width), *weights)
+        cost_estimate=cost,
+        name="late_blocks",
+    )(*operands, *early)
     updated = pl.pallas_call(
         functools.partial(halo_kernel, levels, blocks),
         out_shape=whole,
         in_specs=[vmem] * 12,
         out_specs=hbm,
         scratch_shapes=[
-            pltpu.VMEM((2 * levels, width), BF),
-            pltpu.VMEM((2 * levels, width), BF),
+            pltpu.VMEM((2 * levels, width), F32),
+            pltpu.VMEM((2 * levels, width), F32),
+            pltpu.VMEM((2 * levels, 128), F32),
             pltpu.VMEM((edge_rows, width), BF),
             pltpu.SemaphoreType.DMA((blocks,)),
         ],
         compiler_params=pltpu.CompilerParams(vmem_limit_bytes=limit),
         name="halo_blocks",
-    )(from_left, from_right, pick, *edge_values, *weights, inner)
+    )(from_left, from_right, pick, *edge_values, w_vqkv, w_vout, w_hqkv, w_hout, inner)
     return updated.reshape(blocks, levels, width)
 
 

time: 10.6 us -> 10.2 us (0.962)
  starting transfers between devices: 5.56 us -> 2.01 us
  Pallas kernels: 3.98 us -> 5.63 us
  waiting for transfers between devices: 0.01 us -> 1.54 us
    ppermute x1, starting transfers between devices: 5.06 us -> 1.56 us  [on_device(): lax.ppermute(to_left, 'tile', [(i, (i - 1) % tiles) for i in range(tiles)])]
    pallas_call x1 -> x2, Pallas kernels: 1.73 us -> 3.62 us  [the longest x1 3.6 us: on_device(): pl.pallas_call(functools.partial(early_kernel, levels), out_shape=results...]
    ppermute x1, waiting for transfers between devices: 0.01 us -> 1.41 us  [on_device(): lax.ppermute(to_right, 'tile', [(i, (i + 1) % tiles) for i in range(tiles)])]
    pallas_call x1, Pallas kernels: 2.25 us -> 2.01 us  [on_device(): pl.pallas_call(functools.partial(halo_kernel, levels, blocks), out_shape=...]
    ppermute x1, waiting for transfers between devices: 0.01 us -> 0.13 us  [on_device(): lax.ppermute(to_left, 'tile', [(i, (i - 1) % tiles) for i in range(tiles)])]
  transfers between devices with their start and end apart: 2 -> 2, of which waited for: 0 -> 2; matrix products, arithmetic and copies ran while one was open for 0% -> 0% of each run, Pallas kernels for 16% -> 36%
where the time goes in v4:
time: 10.2 us; the launch traced here: 10 us
  Pallas kernels  5.63 us (55%)
  starting transfers between devices  2.01 us (20%)
  waiting for transfers between devices  1.54 us (15%)
  local copies, waits for them, and re-layouts  0.81 us (8%)
    pallas_call x1, Pallas kernels, on_device(): pl.pallas_call(functools.partial(early_kernel, levels), out_shape=results...  3.6 us
    pallas_call x1, Pallas kernels, on_device(): pl.pallas_call(functools.partial(halo_kernel, levels, blocks), out_shape=...  2.01 us
    ppermute x1, starting transfers between devices, on_device(): lax.ppermute(to_left, 'tile', [(i, (i - 1) % tiles) for i in range(tiles)])  1.56 us
    ppermute x1, waiting for transfers between devices, on_device(): lax.ppermute(to_right, 'tile', [(i, (i + 1) % tiles) for i in range(tiles)])  1.41 us
    slice x1, local copies, waits for them, and re-layouts, on_device(): edges = [strip[:, c].reshape(rows * levels, width) for c in (CB - 1, 0)]  0.78 us
    ppermute x1, starting transfers between devices, on_device(): lax.ppermute(to_right, 'tile', [(i, (i + 1) % tiles) for i in range(tiles)])  0.45 us
  transfers between devices with their start and end apart: 2, of which 2 were waited for; matrix products, arithmetic and copies ran while one was open for 0% of the time, Pallas kernels for 36%

profile of v4, /device:TPU:0, one launch (start us, length us, event | category | flops | bytes accessed | tf_op | source)
XLA Modules:
  0.0 10.0 jit_solution(18325302132406529149)
XLA Ops:
  0.0 0.8 %fusion = (bf16[2,1,16,512]{3,2,1,0:T(8,128)(2,1)S(1)}, bf16[2,1,16,512]{3,2,1,0:T(8,128)(2,1)S(1)}) fusion(bf16[2,4,16,512]{3,2,1,0:T(8,128)(2,1)} %bitcast.10), kind=kLoop, calls=%fused_computation | loop fusion | bytes 131072 | tf_op jit(solution)/shard_map/slice | solution.py:286
  0.8 0.5 %collective-permute-start = (bf16[32,512]{1,0:T(8,128)(2,1)S(1)}, bf16[32,512]{1,0:T(8,128)(2,1)S(1)}, u32[]{:S(2)}, u32[]{:S(2)}) collective-permute-start(bf16[32,512]{1,0:T(8,128)(2,1)S(1)} %get-tuple-element.20), channel_id=1, source_target_pairs={{0,1},{1,2},{2,3},{3,4},{4,5},{5,6},{6,7},{7,8},{8,9},{9,10},{10,1... | collective-permute-start | bytes 98312 | tf_op jit(solution)/shard_map/ppermute | solution.py:297
  1.2 0.0 copy-start
  1.2 0.0 copy-start.1
  1.2 0.0 copy-start.2
  1.2 0.0 copy-start.3
  1.2 0.0 copy-start.4
  1.3 0.0 copy-start.5
  1.3 3.6 %early_blocks.1 = (bf16[128,512]{1,0:T(8,128)(2,1)S(1)}, bf16[64,512]{1,0:T(8,128)(2,1)S(1)}, bf16[64,512]{1,0:T(8,128)(2,1)S(1)}, f32[64,512]{1,0:T(8,128)S(1)}...) custom-call(bf16[128,512]{1,0:T(8,128)(2,1)} %bitcast.11, ...), custom_call_target="tpu_custom_call", output_to_operand_aliasing={{6}: (6, {})} | custom-call | flops 536870912 | bytes 8388608 | tf_op jit(solution)/shard_map/early_blocks/pallas_call | solution.py:313
  4.9 1.6 %collective-permute-start.1 = (bf16[32,512]{1,0:T(8,128)(2,1)S(1)}, bf16[32,512]{1,0:T(8,128)(2,1)S(1)}, u32[]{:S(2)}, u32[]{:S(2)}) collective-permute-start(bf16[32,512]{1,0:T(8,128)(2,1)S(1)} %get-tuple-element.22), channel_id=1, source_target_pairs={{0,15},{1,0},{2,1},{3,2},{4,3},{5,4},{6,5},{7,6},{8,7},{9,8},{10,9... | collective-permute-start | bytes 98312 | tf_op jit(solution)/shard_map/ppermute | solution.py:325
  6.4 0.0 copy-done
  6.4 0.0 copy-done.1
  6.4 0.0 copy-done.2
  6.4 0.0 copy-done.3
  6.4 0.0 copy-done.4
  6.5 0.0 copy-done.5
  6.5 1.4 %collective-permute-done.from_left = bf16[32,512]{1,0:T(8,128)(2,1)S(1)} collective-permute-done((bf16[32,512]{1,0:T(8,128)(2,1)S(1)}, bf16[32,512]{1,0:T(8,128)(2,1)S(1)}, u32[]{:S(2)}, u32[]{:S(2)}) %collective-permute-start) | collective-permute-done | bytes 32800 | tf_op jit(solution)/shard_map/ppermute | solution.py:297
  7.9 0.1 %collective-permute-done.1.from_right = bf16[32,512]{1,0:T(8,128)(2,1)S(1)} collective-permute-done((bf16[32,512]{1,0:T(8,128)(2,1)S(1)}, bf16[32,512]{1,0:T(8,128)(2,1)S(1)}, u32[]{:S(2)}, u32[]{:S(2)}) %collective-permute-start.1) | collective-permute-done | bytes 32800 | tf_op jit(solution)/shard_map/ppermute | solution.py:325
  8.0 2.0 %halo_blocks.1 = bf16[128,512]{1,0:T(8,128)(2,1)} custom-call(bf16[32,512]{1,0:T(8,128)(2,1)S(1)} %collective-permute-done.from_left, bf16[32,512]{1,0:T(8,128)(2,1)S(1)} %collective-permute-done.1.from_right, f32[2,8,128]{2,1,0:T(8,128)S(1)} %get-tuple-element.29.pick_ref, bf16[64,512]{1,0:T(8,128)(2,1)S(1)} %get-tuple-element.30.mixed_e, ...), custom_call_target="tpu_custom_call" | custom-call | tf_op jit(solution)/shard_map/halo_blocks/pallas_call | solution.py:338
  (2 shorter events, 0.0 us)
Async XLA Ops:
  0.8 7.1 %collective-permute-start = (bf16[32,512]{1,0:T(8,128)(2,1)S(1)}, bf16[32,512]{1,0:T(8,128)(2,1)S(1)}, u32[]{:S(2)}, u32[]{:S(2)}) collective-permute-start(bf16[32,512]{1,0:T(8,128)(2,1)S(1)} %get-tuple-element.20), channel_id=1, source_target_pairs={{0,1},{1,2},{2,3},{3,4},{4,5},{5,6},{6,7},{7,8},{8,9},{9,10},{10,1... | collective-permute-start | bytes 98312 | tf_op jit(solution)/shard_map/ppermute | solution.py:297
  1.2 5.2 %copy-start = (bf16[512,1536]{1,0:T(8,128)(2,1)S(1)}, bf16[512,1536]{1,0:T(8,128)(2,1)}, u32[]{:S(2)}) copy-start(bf16[512,1536]{1,0:T(8,128)(2,1)} %w_vqkv.1) | copy-start | bytes 4718596
  1.2 5.2 %copy-start.1 = (bf16[512,1536]{1,0:T(8,128)(2,1)S(1)}, bf16[512,1536]{1,0:T(8,128)(2,1)}, u32[]{:S(2)}) copy-start(bf16[512,1536]{1,0:T(8,128)(2,1)} %w_hqkv.1) | copy-start | bytes 4718596
  1.2 5.2 %copy-start.2 = (bf16[512,512]{1,0:T(8,128)(2,1)S(1)}, bf16[512,512]{1,0:T(8,128)(2,1)}, u32[]{:S(2)}) copy-start(bf16[512,512]{1,0:T(8,128)(2,1)} %w_vout.1) | copy-start | bytes 1572868
  1.2 5.2 %copy-start.3 = (bf16[512,512]{1,0:T(8,128)(2,1)S(1)}, bf16[512,512]{1,0:T(8,128)(2,1)}, u32[]{:S(2)}) copy-start(bf16[512,512]{1,0:T(8,128)(2,1)} %w_hout.1) | copy-start | bytes 1572868
  1.2 5.2 %copy-start.4 = (bf16[8,16,512]{2,1,0:T(8,128)(2,1)S(1)}, bf16[8,16,512]{2,1,0:T(8,128)(2,1)}, u32[]{:S(2)}) copy-start(bf16[8,16,512]{2,1,0:T(8,128)(2,1)} %param.6) | copy-start | bytes 393220
  1.3 5.2 %copy-start.5 = (s32[128]{0:T(128)S(1)}, s32[128]{0:T(128)}, u32[]{:S(2)}) copy-start(s32[128]{0:T(128)} %param.7) | copy-start | bytes 1540
  4.9 3.2 %collective-permute-start.1 = (bf16[32,512]{1,0:T(8,128)(2,1)S(1)}, bf16[32,512]{1,0:T(8,128)(2,1)S(1)}, u32[]{:S(2)}, u32[]{:S(2)}) collective-permute-start(bf16[32,512]{1,0:T(8,128)(2,1)S(1)} %get-tuple-element.22), channel_id=1, source_target_pairs={{0,15},{1,0},{2,1},{3,2},{4,3},{5,4},{6,5},{7,6},{8,7},{9,8},{10,9... | collective-permute-start | bytes 98312 | tf_op jit(solution)/shard_map/ppermute | solution.py:325
